TPU v7x, 512 devices: a whole 4x4x16 slice. The times are simulated.
512 devices in a mesh: stab: 16 (over z), round: 8 (over y, x_lo), shot: 4 (over x_hi, core).
Axes of the slice: x: 4 (x_hi: 2, x_lo: 2; x = x_hi * 2 + x_lo), y: 4, z: 16, core: 2. Of those that a mesh axis runs over, the one named last changes fastest.
Arguments:
- states_in: bfloat16 [8, 64, 624, 256], P('shot', 'round', 'stab'), parts along dimension 0, may hold values from -6 to 6
- bits: int32 [8, 64, 624], P('shot', 'round', 'stab'), parts along dimension 0, may hold values 0 or 1
- coords: int32 [64, 624], P('round', 'stab'), may hold values from 0 to 624
- coord_table: bfloat16 [625, 256], replicated, may hold values from -8 to 8
- flip_embed: bfloat16 [256], replicated, may hold values from -6 to 6
- gain_attn: bfloat16 [256], replicated, may hold values from 0.25 to 1.75
- w_query: bfloat16 [256, 256], replicated, may hold values from -1 to 1
- w_key: bfloat16 [256, 256], replicated, may hold values from -1 to 1
- w_value: bfloat16 [256, 256], replicated, may hold values from -0.375 to 0.375
- w_out: bfloat16 [256, 256], replicated, may hold values from -0.375 to 0.375
- gain_rec: bfloat16 [256], replicated, may hold values from 0.25 to 1.75
- w_decay: bfloat16 [256, 256], replicated, may hold values from -0.375 to 0.375
- decay_bias: float32 [256], replicated, may hold values from -1 to 6
- w_input: bfloat16 [256, 256], replicated, may hold values from -0.375 to 0.375
- w_rec_out: bfloat16 [256, 256], replicated, may hold values from -0.375 to 0.375
- gain_mlp: bfloat16 [256], replicated, may hold values from 0.25 to 1.75
- w_gate: bfloat16 [256, 1024], replicated, may hold values from -0.375 to 0.375
- w_up: bfloat16 [256, 1024], replicated, may hold values from -0.375 to 0.375
- w_down: bfloat16 [1024, 256], replicated, may hold values from -0.1875 to 0.1875
Outputs:
- states: bfloat16 [8, 64, 624, 256], P('shot', 'round', 'stab'), parts along dimension 0
There are 4 independent parts, one for each index of `shot`. A program takes and returns all parts, laid end to end along the dimension named above; an argument that names none is the same for every part. Nothing has to cross between parts.
All inputs are finite; a program needn't handle non-finite values. No bound on the sum of `bits` on one device may be relied on, other than what follows from the above.
Results may differ from a plain program's by a relative error of at most 0.0065.
Values may be sent and summed in bfloat16 or wider, within the bound.
A program may use at most 128 MiB of HBM per device.

v0:
```python
import jax
import jax.numpy as jnp
from jax import lax
from jax.sharding import PartitionSpec as P

HD = 32


def shifted(value, axis, steps):
    count = lax.axis_size(axis)
    initial, last = (max(0, -steps), min(count, count - steps))
    return lax.ppermute(value, axis, [(source, source + steps) for source in range(initial, last)])


def norm_rows(values, gain):
    scale = lax.rsqrt(jnp.mean(values * values, axis=-1, keepdims=True) + 1e-05)
    return (values * scale * gain.astype(jnp.float32)).astype(jnp.bfloat16)


def project(left, right):
    return jnp.dot(left, right, preferred_element_type=jnp.float32)


def softmax_step(carry, query, key_piece, value_piece):
    run_max, run_total, run_acc = carry
    scores = jnp.einsum(
        "brqhe,brkhe->brhqk", query, key_piece, preferred_element_type=jnp.float32
    ) * HD ** (-0.5)
    new_max = jnp.maximum(run_max, jnp.max(scores, axis=-1))
    expo = jnp.exp(scores - new_max[..., None])
    run_total = jnp.sum(expo, axis=-1)
    product = jnp.einsum(
        "brhqk,brkhe->brqhe",
        expo.astype(jnp.bfloat16),
        value_piece,
        preferred_element_type=jnp.float32,
    )
    run_acc = product
    return (new_max, run_total, run_acc)


def body(
    states_in,
    bits,
    coords,
    coord_table,
    flip_embed,
    gain_attn,
    w_query,
    w_key,
    w_value,
    w_out,
    gain_rec,
    w_decay,
    decay_bias,
    w_input,
    w_rec_out,
    gain_mlp,
    w_gate,
    w_up,
    w_down,
):
    shots, rounds, stabs = bits.shape
    width = coord_table.shape[1]
    heads = width // HD
    base = jnp.take(coord_table, coords, axis=0).astype(jnp.float32)
    signs = (2 * bits - 1).astype(jnp.float32)[..., None]
    start = states_in.astype(jnp.float32) + base[None] + signs * flip_embed.astype(jnp.float32)
    normed = norm_rows(start, gain_attn)
    query = project(normed, w_query).astype(jnp.bfloat16).reshape(shots, rounds, stabs, heads, HD)
    first_max = jnp.full((shots, rounds, heads, stabs), -1e30, jnp.float32)
    first_total = jnp.zeros((shots, rounds, heads, stabs), jnp.float32)
    first_acc = jnp.zeros((shots, rounds, stabs, heads, HD), jnp.float32)
    initial = (first_max, first_total, first_acc)
    keys = project(normed, w_key).astype(jnp.bfloat16)
    values = project(normed, w_value).astype(jnp.bfloat16)
    pieces = (
        lax.all_gather(keys, "stab", axis=2, tiled=True),
        lax.all_gather(values, "stab", axis=2, tiled=True),
    )
    count = pieces[0].shape[2]
    key_piece = pieces[0].reshape(shots, rounds, count, heads, HD)
    value_piece = pieces[1].reshape(shots, rounds, count, heads, HD)
    result = softmax_step(initial, query, key_piece, value_piece)
    final_total = jnp.transpose(result[1], (0, 1, 3, 2))[..., None]
    mixed = (result[2] / final_total).astype(jnp.bfloat16).reshape(shots, rounds, stabs, width)
    after_attn = start + project(mixed, w_out)
    rec_in = norm_rows(after_attn, gain_rec)
    decay = jax.nn.sigmoid(project(rec_in, w_decay) + decay_bias)
    drive = (1.0 - decay) * project(rec_in, w_input)

    def advance(state, inputs):
        local_state, product = state
        local_state = inputs[0] * local_state + inputs[1]
        product = product * inputs[0]
        return ((local_state, product), (local_state, product))

    zero_state = jnp.zeros((shots, stabs, width), jnp.float32)
    unit_state = jnp.ones((shots, stabs, width), jnp.float32)
    ending, history = lax.scan(
        advance, (zero_state, unit_state), (jnp.moveaxis(decay, 1, 0), jnp.moveaxis(drive, 1, 0))
    )
    last_state, last_product = ending

    def relay_step(step, entering):
        return shifted(
            (last_product * entering + last_state).astype(jnp.bfloat16), "round", 1
        ).astype(jnp.float32)

    incoming = lax.fori_loop(0, lax.axis_size("round") - 1, relay_step, zero_state)
    hidden = history[0] + history[1] * incoming[None]
    hidden = jnp.moveaxis(hidden, 0, 1)
    after_rec = after_attn + project(hidden.astype(jnp.bfloat16), w_rec_out)
    ffn_in = norm_rows(after_rec, gain_mlp)
    inner = (jax.nn.silu(project(ffn_in, w_gate)) * project(ffn_in, w_up)).astype(jnp.bfloat16)
    return (after_rec + project(inner, w_down)).astype(jnp.bfloat16)


def solution(mesh):
    placed = (
        P("shot", "round", "stab", None),
        P("shot", "round", "stab"),
        P("round", "stab"),
        P(),
        P(),
        P(),
        P(),
        P(),
        P(),
        P(),
        P(),
        P(),
        P(),
        P(),
        P(),
        P(),
        P(),
        P(),
        P(),
    )
    return jax.shard_map(
        body,
        mesh=mesh,
        in_specs=placed,
        out_specs=P("shot", "round", "stab", None),
        check_vma=False,
    )
```

profile of v0, /device:TPU:24, one launch (start us, length us, event | category | flops | bytes accessed | tf_op | source)
XLA Modules:
  0.0 271.2 jit_solution(17156289981482771715)
XLA Ops:
  8.1 2.6 gather_fusion
  19.4 83.2 %all-gather.5.cloned.1.call-done = bf16[2,8,624,256]{3,1,0,2:T(8,128)(2,1)} async-done(((bf16[2,8,39,256]{3,1,0,2:T(8,128)(2,1)}), bf16[2,8,624,256]{3,1,0,2:T(8,128)(2,1)}) %all-gather.5.cloned.1.call-update) | async-done | bytes 5111824 | tf_op jit(solution)/shard_map/all_gather | solution.py:78
  102.6 8.9 %copy.44 = bf16[2,8,624,256]{2,3,1,0:T(8,128)(2,1)} copy(bf16[2,8,624,256]{3,1,0,2:T(8,128)(2,1)} %all-gather.5.cloned.1.call-done) | data formatting | bytes 10223616 | tf_op jit(solution)/shard_map/all_gather | solution.py:78
  111.5 4.4 %multiply_reduce_fusion = (f32[2,8,8,39]{3,2,1,0:T(8,128)S(1)}, f32[2,8,8,39,624]{4,3,2,1,0:T(8,128)S(1)}) fusion(bf16[2,8,39,8,32]{2,4,3,1,0:T(8,128)(2,1)S(1)} %bitcast.103, bf16[2,8,624,8,32]{2,4,3,1,0:T(8,128)(2,1)} %bitcast.101), kind=kOutput, calls=%fused_computation.10 | convolution fusion | flops 205585536 | bytes 17911296 | tf_op jit(solution)/shard_map/brqhe,brkhe->brhqk/dot_general | solution.py:26
  116.0 4.7 %copy-done.1 = f32[2,8,8,39,624]{4,3,2,1,0:T(8,128)} copy-done((f32[2,8,8,39,624]{4,3,2,1,0:T(8,128)}, f32[2,8,8,39,624]{4,3,2,1,0:T(8,128)S(1)}, u32[]{:S(2)}) %copy-start.1) | copy-done | bytes 12460056
  120.7 3.3 %fusion.2 = f32[2,8,8,39]{3,2,1,0:T(8,128)S(1)} fusion(f32[2,8,8,39,624]{4,3,2,1,0:T(8,128)S(1)} %get-tuple-element.161, f32[2,8,8,39]{3,2,1,0:T(8,128)S(1)} %broadcast_maximum_fusion), kind=kLoop, calls=%fused_computation.11 | loop fusion | flops 9340032 | bytes 12499968 | tf_op jit(solution)/shard_map/reduce_sum | solution.py:31
  124.0 57.2 %all-gather.3.cloned.1.call-done = bf16[2,8,624,256]{3,1,0,2:T(8,128)(2,1)} async-done(((bf16[2,8,39,256]{3,1,0,2:T(8,128)(2,1)}), bf16[2,8,624,256]{3,1,0,2:T(8,128)(2,1)}) %all-gather.3.cloned.1.call-update) | async-done | bytes 5111824 | tf_op jit(solution)/shard_map/all_gather | solution.py:79
  181.2 8.9 %copy.41 = bf16[2,8,624,256]{2,3,1,0:T(8,128)(2,1)} copy(bf16[2,8,624,256]{3,1,0,2:T(8,128)(2,1)} %all-gather.3.cloned.1.call-done) | data formatting | bytes 10223616 | tf_op jit(solution)/shard_map/all_gather | solution.py:79
  190.1 10.0 %fusion.8 = bf16[2,8,39,8,32]{2,4,3,1,0:T(8,128)(2,1)} fusion(bf16[2,8,624,8,32]{2,4,3,1,0:T(8,128)(2,1)} %bitcast.102, f32[2,8,8,39,624]{4,3,2,1,0:T(8,128)} %copy-done.1, f32[2,8,8,39]{3,2,1,0:T(8,128)S(1)} %broadcast_maximum_fusion, f32[2,8,39,8]{2,3,1,0:T(8,128)S(1)} %bitcast.105), kind=kOutput, calls=%fused_computation.18 | convolution fusion | flops 209025024 | bytes 17931264 | tf_op jit(solution)/shard_map/brhqk,brkhe->brqhe/dot_general | solution.py:32
  202.7 5.5 %while.28 = (s32[]{:T(128)}, f32[2,39,256]{2,1,0:T(8,128)S(1)}, f32[2,39,256]{2,1,0:T(8,128)S(1)}, f32[8,2,39,256]{3,2,1,0:T(8,128)S(1)}, f32[8,2,39,256]{3,2,1,...) while((s32[]{:T(128)}, f32[2,39,256]{2,1,0:T(8,128)S(1)}, ...), condition=%wide.region_5.6_spmd.clone, body=%wide.region_4.5_spmd.clone.sunk | while | flops 99843 | bytes 655975 | solution.py:100
  208.2 48.1 %while.29 = (s32[]{:T(128)}, f32[2,39,256]{2,1,0:T(8,128)S(1)}, f32[2,39,256]{2,1,0:T(8,128)S(1)}, f32[2,39,256]{2,1,0:T(8,128)S(1)}, s32[]{:T(128)}, /*index=5*/s32[]{:T(128)}) while((s32[]{:T(128)}, f32[2,39,256]{2,1,0:T(8,128)S(1)}, f32[2,39,256]{2,1,0:T(8,128)S(1)}, f32[2,39,256]{2,1,0:T(8,128)S(1)}, s32[]{:T(128)}, ...), condition=%wide.region_7.8_spmd.clone, body=%wide.region_6.7_spmd.clone.sunk | while | flops 99843 | bytes 559223 | solution.py:110
  208.2 3.5 %collective-permute-start = (bf16[2,39,256]{2,1,0:T(8,128)(2,1)S(1)}, bf16[2,39,256]{2,1,0:T(8,128)(2,1)S(1)}, u32[]{:S(2)}, u32[]{:S(2)}) collective-permute-start(bf16[2,39,256]{2,1,0:T(8,128)(2,1)S(1)} %fusion.50), channel_id=1, source_target_pairs={{0,4},{4,8},{8,12},{12,16},{16,20},{20,24},{24,28},{1,5},{5,9},{9,... | collective-permute-start | bytes 119816 | tf_op jit(solution)/shard_map/while/body/eval_jaxpr/ppermute | solution.py:12
  211.7 3.3 %collective-permute-done = bf16[2,39,256]{2,1,0:T(8,128)(2,1)S(1)} collective-permute-done((bf16[2,39,256]{2,1,0:T(8,128)(2,1)S(1)}, bf16[2,39,256]{2,1,0:T(8,128)(2,1)S(1)}, u32[]{:S(2)}, u32[]{:S(2)}) %collective-permute-start) | collective-permute-done | bytes 39968 | tf_op jit(solution)/shard_map/while/body/eval_jaxpr/ppermute | solution.py:12
  215.1 2.6 collective-permute-start
  217.7 4.2 %collective-permute-done = bf16[2,39,256]{2,1,0:T(8,128)(2,1)S(1)} collective-permute-done((bf16[2,39,256]{2,1,0:T(8,128)(2,1)S(1)}, bf16[2,39,256]{2,1,0:T(8,128)(2,1)S(1)}, u32[]{:S(2)}, u32[]{:S(2)}) %collective-permute-start) | collective-permute-done | bytes 39968 | tf_op jit(solution)/shard_map/while/body/eval_jaxpr/ppermute | solution.py:12
  221.9 1.9 collective-permute-start
  223.8 4.9 %collective-permute-done = bf16[2,39,256]{2,1,0:T(8,128)(2,1)S(1)} collective-permute-done((bf16[2,39,256]{2,1,0:T(8,128)(2,1)S(1)}, bf16[2,39,256]{2,1,0:T(8,128)(2,1)S(1)}, u32[]{:S(2)}, u32[]{:S(2)}) %collective-permute-start) | collective-permute-done | bytes 39968 | tf_op jit(solution)/shard_map/while/body/eval_jaxpr/ppermute | solution.py:12
  230.7 5.1 %collective-permute-done = bf16[2,39,256]{2,1,0:T(8,128)(2,1)S(1)} collective-permute-done((bf16[2,39,256]{2,1,0:T(8,128)(2,1)S(1)}, bf16[2,39,256]{2,1,0:T(8,128)(2,1)S(1)}, u32[]{:S(2)}, u32[]{:S(2)}) %collective-permute-start) | collective-permute-done | bytes 39968 | tf_op jit(solution)/shard_map/while/body/eval_jaxpr/ppermute | solution.py:12
  237.8 4.9 %collective-permute-done = bf16[2,39,256]{2,1,0:T(8,128)(2,1)S(1)} collective-permute-done((bf16[2,39,256]{2,1,0:T(8,128)(2,1)S(1)}, bf16[2,39,256]{2,1,0:T(8,128)(2,1)S(1)}, u32[]{:S(2)}, u32[]{:S(2)}) %collective-permute-start) | collective-permute-done | bytes 39968 | tf_op jit(solution)/shard_map/while/body/eval_jaxpr/ppermute | solution.py:12
  242.7 1.9 collective-permute-start
  244.6 4.9 %collective-permute-done = bf16[2,39,256]{2,1,0:T(8,128)(2,1)S(1)} collective-permute-done((bf16[2,39,256]{2,1,0:T(8,128)(2,1)S(1)}, bf16[2,39,256]{2,1,0:T(8,128)(2,1)S(1)}, u32[]{:S(2)}, u32[]{:S(2)}) %collective-permute-start) | collective-permute-done | bytes 39968 | tf_op jit(solution)/shard_map/while/body/eval_jaxpr/ppermute | solution.py:12
  249.5 1.9 collective-permute-start
  251.5 4.9 %collective-permute-done = bf16[2,39,256]{2,1,0:T(8,128)(2,1)S(1)} collective-permute-done((bf16[2,39,256]{2,1,0:T(8,128)(2,1)S(1)}, bf16[2,39,256]{2,1,0:T(8,128)(2,1)S(1)}, u32[]{:S(2)}, u32[]{:S(2)}) %collective-permute-start) | collective-permute-done | bytes 39968 | tf_op jit(solution)/shard_map/while/body/eval_jaxpr/ppermute | solution.py:12
  259.2 3.4 %fusion.17 = bf16[2,8,39,256]{3,2,1,0:T(8,128)(2,1)} fusion(f32[2,8,39,256]{3,2,1,0:T(8,128)} %copy-done.3, f32[2,8,39,1024]{3,2,1,0:T(8,128)S(1)} %fusion.21, bf16[1024,256]{1,0:T(8,128)(2,1)} %param.41, bf16[256,1024]{1,0:T(8,128)(2,1)} %param.40, f32[256]{0:T(256)S(1)} %convert_element_type.82, f32[2,8,39]{2,1,0:T(8,128)S(1)} %add_rsqrt_fusion), kind=kOutput, calls=%fused_computation.30 | convolution fusion | flops 658944000 | bytes 4566464 | tf_op jit(solution)/shard_map/dot_general | solution.py:21
  (85 shorter events, 26.8 us)
Async XLA Ops:
  6.5 252.1 %copy-start = (bf16[256,1024]{1,0:T(8,128)(2,1)S(1)}, bf16[256,1024]{1,0:T(8,128)(2,1)}, u32[]{:S(2)}) copy-start(bf16[256,1024]{1,0:T(8,128)(2,1)} %param.39) | copy-start | bytes 1572868
  6.5 11.0 %copy-start.5 = (bf16[256,256]{1,0:T(8,128)(2,1)S(1)}, bf16[256,256]{1,0:T(8,128)(2,1)}, u32[]{:S(2)}) copy-start(bf16[256,256]{1,0:T(8,128)(2,1)} %param.31) | copy-start | bytes 393220
  6.5 12.1 %copy-start.6 = (bf16[256,256]{1,0:T(8,128)(2,1)S(1)}, bf16[256,256]{1,0:T(8,128)(2,1)}, u32[]{:S(2)}) copy-start(bf16[256,256]{1,0:T(8,128)(2,1)} %param.29) | copy-start | bytes 393220
  6.5 12.9 %copy-start.10 = (bf16[256]{0:T(256)(128)(2,1)S(1)}, bf16[256]{0:T(256)(128)(2,1)}, u32[]{:S(2)}) copy-start(bf16[256]{0:T(256)(128)(2,1)} %param.33) | copy-start | bytes 1540
  6.5 12.9 %copy-start.11 = (bf16[256]{0:T(256)(128)(2,1)S(1)}, bf16[256]{0:T(256)(128)(2,1)}, u32[]{:S(2)}) copy-start(bf16[256]{0:T(256)(128)(2,1)} %param.38) | copy-start | bytes 1540
  6.5 96.1 %all-gather.5.cloned.1.call-start = ((), (), s32[]{:S(2)}) async-start(), calls=%async_computation.1 | async-start | bytes 5431296 | tf_op jit(solution)/shard_map/all_gather | solution.py:78
  17.5 163.7 %all-gather.3.cloned.1.call-start = ((), (), s32[]{:S(2)}) async-start(), calls=%async_computation | async-start | bytes 5431296 | tf_op jit(solution)/shard_map/all_gather | solution.py:79
  116.0 4.7 %copy-start.1 = (f32[2,8,8,39,624]{4,3,2,1,0:T(8,128)}, f32[2,8,8,39,624]{4,3,2,1,0:T(8,128)S(1)}, u32[]{:S(2)}) copy-start(f32[2,8,8,39,624]{4,3,2,1,0:T(8,128)S(1)} %get-tuple-element.161) | copy-start | bytes 37380100
  190.1 10.0 %copy-start.2 = (bf16[2,8,39,256]{3,1,2,0:T(8,128)(2,1)S(1)}, bf16[2,8,39,256]{3,1,2,0:T(8,128)(2,1)}, u32[]{:S(2)}) copy-start(bf16[2,8,39,256]{3,1,2,0:T(8,128)(2,1)} %param.23) | copy-start | bytes 958468
  190.1 10.0 %copy-start.4 = (bf16[256,256]{1,0:T(8,128)(2,1)S(1)}, bf16[256,256]{1,0:T(8,128)(2,1)}, u32[]{:S(2)}) copy-start(bf16[256,256]{1,0:T(8,128)(2,1)} %param.32) | copy-start | bytes 393220
  190.1 11.8 %copy-start.8 = (bf16[256,256]{1,0:T(8,128)(2,1)S(1)}, bf16[256,256]{1,0:T(8,128)(2,1)}, u32[]{:S(2)}) copy-start(bf16[256,256]{1,0:T(8,128)(2,1)} %param.34) | copy-start | bytes 393220
  190.1 11.9 %copy-start.9 = (f32[256]{0:T(256)S(1)}, f32[256]{0:T(256)}, u32[]{:S(2)}) copy-start(f32[256]{0:T(256)} %param.35) | copy-start | bytes 3076
  200.0 2.3 copy-start.7
  208.2 6.8 %collective-permute-start = (bf16[2,39,256]{2,1,0:T(8,128)(2,1)S(1)}, bf16[2,39,256]{2,1,0:T(8,128)(2,1)S(1)}, u32[]{:S(2)}, u32[]{:S(2)}) collective-permute-start(bf16[2,39,256]{2,1,0:T(8,128)(2,1)S(1)} %fusion.50), channel_id=1, source_target_pairs={{0,4},{4,8},{8,12},{12,16},{16,20},{20,24},{24,28},{1,5},{5,9},{9,... | collective-permute-start | bytes 119816 | tf_op jit(solution)/shard_map/while/body/eval_jaxpr/ppermute | solution.py:12
  215.1 6.8 %collective-permute-start = (bf16[2,39,256]{2,1,0:T(8,128)(2,1)S(1)}, bf16[2,39,256]{2,1,0:T(8,128)(2,1)S(1)}, u32[]{:S(2)}, u32[]{:S(2)}) collective-permute-start(bf16[2,39,256]{2,1,0:T(8,128)(2,1)S(1)} %fusion.50), channel_id=1, source_target_pairs={{0,4},{4,8},{8,12},{12,16},{16,20},{20,24},{24,28},{1,5},{5,9},{9,... | collective-permute-start | bytes 119816 | tf_op jit(solution)/shard_map/while/body/eval_jaxpr/ppermute | solution.py:12
  221.9 6.8 %collective-permute-start = (bf16[2,39,256]{2,1,0:T(8,128)(2,1)S(1)}, bf16[2,39,256]{2,1,0:T(8,128)(2,1)S(1)}, u32[]{:S(2)}, u32[]{:S(2)}) collective-permute-start(bf16[2,39,256]{2,1,0:T(8,128)(2,1)S(1)} %fusion.50), channel_id=1, source_target_pairs={{0,4},{4,8},{8,12},{12,16},{16,20},{20,24},{24,28},{1,5},{5,9},{9,... | collective-permute-start | bytes 119816 | tf_op jit(solution)/shard_map/while/body/eval_jaxpr/ppermute | solution.py:12
  228.8 7.0 %collective-permute-start = (bf16[2,39,256]{2,1,0:T(8,128)(2,1)S(1)}, bf16[2,39,256]{2,1,0:T(8,128)(2,1)S(1)}, u32[]{:S(2)}, u32[]{:S(2)}) collective-permute-start(bf16[2,39,256]{2,1,0:T(8,128)(2,1)S(1)} %fusion.50), channel_id=1, source_target_pairs={{0,4},{4,8},{8,12},{12,16},{16,20},{20,24},{24,28},{1,5},{5,9},{9,... | collective-permute-start | bytes 119816 | tf_op jit(solution)/shard_map/while/body/eval_jaxpr/ppermute | solution.py:12
  235.8 6.8 %collective-permute-start = (bf16[2,39,256]{2,1,0:T(8,128)(2,1)S(1)}, bf16[2,39,256]{2,1,0:T(8,128)(2,1)S(1)}, u32[]{:S(2)}, u32[]{:S(2)}) collective-permute-start(bf16[2,39,256]{2,1,0:T(8,128)(2,1)S(1)} %fusion.50), channel_id=1, source_target_pairs={{0,4},{4,8},{8,12},{12,16},{16,20},{20,24},{24,28},{1,5},{5,9},{9,... | collective-permute-start | bytes 119816 | tf_op jit(solution)/shard_map/while/body/eval_jaxpr/ppermute | solution.py:12
  242.7 6.8 %collective-permute-start = (bf16[2,39,256]{2,1,0:T(8,128)(2,1)S(1)}, bf16[2,39,256]{2,1,0:T(8,128)(2,1)S(1)}, u32[]{:S(2)}, u32[]{:S(2)}) collective-permute-start(bf16[2,39,256]{2,1,0:T(8,128)(2,1)S(1)} %fusion.50), channel_id=1, source_target_pairs={{0,4},{4,8},{8,12},{12,16},{16,20},{20,24},{24,28},{1,5},{5,9},{9,... | collective-permute-start | bytes 119816 | tf_op jit(solution)/shard_map/while/body/eval_jaxpr/ppermute | solution.py:12
  249.5 6.8 %collective-permute-start = (bf16[2,39,256]{2,1,0:T(8,128)(2,1)S(1)}, bf16[2,39,256]{2,1,0:T(8,128)(2,1)S(1)}, u32[]{:S(2)}, u32[]{:S(2)}) collective-permute-start(bf16[2,39,256]{2,1,0:T(8,128)(2,1)S(1)} %fusion.50), channel_id=1, source_target_pairs={{0,4},{4,8},{8,12},{12,16},{16,20},{20,24},{24,28},{1,5},{5,9},{9,... | collective-permute-start | bytes 119816 | tf_op jit(solution)/shard_map/while/body/eval_jaxpr/ppermute | solution.py:12
  257.8 0.8 copy-start.3
Sparse Core Ops, SparseCore 0:
  17.6 84.9 all-gather.4
  104.7 76.4 all-gather.2
where the time goes:
time: 273 us; the launch traced here: 271 us
  waiting for transfers between devices  173 us (63%)
  local copies, waits for them, and re-layouts  29.9 us (11%)
  matrix products  24 us (9%)
  starting transfers between devices  15.7 us (6%)
  other arithmetic  15.1 us (6%)
  between operations  13.7 us (5%)
    all_gather x1, waiting for transfers between devices, body(): lax.all_gather(keys, 'stab', axis=2, tiled=True)  83.2 us
    all_gather x1, waiting for transfers between devices, body(): lax.all_gather(values, 'stab', axis=2, tiled=True)  57.2 us
    ppermute x7, waiting for transfers between devices, shifted(): lax.ppermute(value, axis, [(source, source + steps) for source in range(i...  32.1 us
    ppermute x7, starting transfers between devices, shifted(): lax.ppermute(value, axis, [(source, source + steps) for source in range(i...  15.7 us
    dot_general x1, matrix products, softmax_step(): jnp.einsum('brhqk,brkhe->brqhe', expo.astype(jnp.bfloat16), value_piece,...  9.95 us
    dot_general x9, matrix products, project(): return jnp.dot(left, right, preferred_element_type=jnp.float32)  9.64 us
    all_gather x1, local copies, waits for them, and re-layouts, body(): lax.all_gather(keys, 'stab', axis=2, tiled=True)  8.89 us
    all_gather x1, local copies, waits for them, and re-layouts, body(): lax.all_gather(values, 'stab', axis=2, tiled=True)  8.87 us
  transfers between devices with their start and end apart: 9, of which 9 were waited for; matrix products, arithmetic and copies ran while one was open for 7% of the time, Pallas kernels for 0%

commit v1 on v0

v1 whole, which is shorter than its diff:
```python
import functools

import jax
import jax.numpy as jnp
from jax import lax
from jax.experimental import pallas as pl
from jax.experimental.pallas import tpu as pltpu
from jax.sharding import PartitionSpec as P

HD = 32
LANES = 128
GROUP = 4
MESH = pl.DeviceIdType.MESH
F32 = jnp.float32
BF16 = jnp.bfloat16


def dot(left, right):
    return jnp.dot(left, right, preferred_element_type=F32)


def dot_t(left, right):
    return lax.dot_general(left, right, (((1,), (1,)), ((), ())), preferred_element_type=F32)


def norm_rows(values, gain):
    scale = lax.rsqrt(jnp.mean(values * values, axis=-1, keepdims=True) + 1e-05)
    return values * scale * gain


def pack(rows):
    return jnp.concatenate([rows[:, :LANES], rows[:, LANES:]], axis=0).astype(BF16)


def unpack(message):
    wide = message.astype(F32)
    half = wide.shape[0] // 2
    return jnp.concatenate([wide[:half], wide[half:]], axis=1)


def hop(slot):
    return (slot + 1) // 2 if slot % 2 else -(slot // 2)


def kernel(
    parts,
    blocks,
    states_ref,
    bits_ref,
    coords_ref,
    table_ref,
    flip_ref,
    gain_attn_ref,
    wq_ref,
    wk_ref,
    wv_ref,
    wo_ref,
    gain_rec_ref,
    wd_ref,
    bias_ref,
    wi_ref,
    wr_ref,
    gain_mlp_ref,
    wg_ref,
    wu_ref,
    wdown_ref,
    out_ref,
    small_ref,
    start_ref,
    send1,
    recv1,
    q_ref,
    k_ref,
    v_ref,
    send2,
    recv2,
    after_ref,
    decay_ref,
    drive_ref,
    send3,
    recv3,
    inc_ref,
    send1_sem,
    recv1_sem,
    send2_sem,
    recv2_sem,
    send3_sem,
    recv3_sem,
):
    shots, rounds, stabs, width = states_ref.shape
    rows = start_ref.shape[1]
    coord_rows = table_ref.shape[0]
    heads = width // HD
    gsize = GROUP * rows
    groups = parts // GROUP
    keys = parts * rows
    me = lax.axis_index("stab")
    block = lax.axis_index("round")

    def peer(offset):
        return lax.rem(me + (offset + parts), parts)

    barrier = pltpu.get_barrier_semaphore()
    for offset in range(1, parts):
        pl.semaphore_signal(barrier, inc=1, device_id={"stab": peer(offset)}, device_id_type=MESH)
    for offset in range(1, blocks):
        pl.semaphore_signal(
            barrier, inc=1, device_id={"round": lax.rem(block + offset, blocks)}, device_id_type=MESH
        )

    small_ref[...] = jnp.zeros_like(small_ref)
    small_ref[0:rounds, 0:stabs] = coords_ref[...].astype(F32)
    for shot in range(shots):
        first = rounds * (1 + shot)
        small_ref[first : first + rounds, 0:stabs] = bits_ref[shot].astype(F32)
    turned = jnp.transpose(small_ref[...])
    small_ref[...] = turned
    small_ref[stabs : stabs + 1, :] = small_ref[stabs - 1 : stabs, :]
    flip = flip_ref[...].astype(F32)
    gain_attn = gain_attn_ref[...].astype(F32)
    spot = lax.broadcasted_iota(jnp.int32, (rows, coord_rows), 1).astype(F32)
    for pair in range(rounds // 2):
        picks = []
        for t in (2 * pair, 2 * pair + 1):
            picks.append(jnp.where(small_ref[0:rows, t : t + 1] == spot, 1.0, 0.0))
        base = dot(jnp.concatenate(picks, axis=0).astype(BF16), table_ref[...])
        for half in range(2):
            t = 2 * pair + half
            for shot in range(shots):
                item = shot * rounds + t
                lane = rounds * (1 + shot) + t
                own = states_ref[shot, t].astype(F32)
                start_ref[item, 0:stabs, :] = own
                start_ref[item, stabs : stabs + 1, :] = own[stabs - 1 : stabs, :]
                sign = 2.0 * small_ref[0:rows, lane : lane + 1] - 1.0
                start = start_ref[item] + base[half * rows : (half + 1) * rows] + sign * flip
                start_ref[item] = start
                send1[item] = pack(norm_rows(start, gain_attn))

    pl.semaphore_wait(barrier, parts - 1 + blocks - 1)

    def copy1(slot):
        offset = hop(slot)
        back = slot if slot in (0, parts - 1) else (slot + 1 if slot % 2 else slot - 1)
        return pltpu.make_async_remote_copy(
            src_ref=send1.at[peer(offset)],
            dst_ref=recv1.at[back],
            send_sem=send1_sem.at[slot],
            recv_sem=recv1_sem.at[back],
            device_id={"stab": peer(offset)},
            device_id_type=MESH,
        )

    for slot in range(parts - 1, 0, -1):
        copy1(slot).start()
    recv1[0] = send1[me]

    real = lax.rem(lax.broadcasted_iota(jnp.int32, (gsize, 1), 0), rows) < stabs
    for group in range(groups):
        pieces = []
        for slot in range(group * GROUP, (group + 1) * GROUP):
            if slot:
                pltpu.make_async_remote_copy(
                    src_ref=send1.at[0],
                    dst_ref=recv1.at[slot],
                    send_sem=send1_sem.at[slot],
                    recv_sem=recv1_sem.at[slot],
                    device_id={"stab": peer(1)},
                    device_id_type=MESH,
                ).wait_recv()
            pieces.append(unpack(recv1[slot]))
        normed = jnp.concatenate(pieces, axis=0).astype(BF16)
        where = slice(group * gsize, (group + 1) * gsize)
        q_ref[where, :] = dot(normed, wq_ref[...]).astype(BF16)
        k_ref[where, :] = dot(normed, wk_ref[...]).astype(BF16)
        value = dot(normed, wv_ref[...])
        head_of = lax.broadcasted_iota(jnp.int32, (gsize, width), 1) // HD
        for head in range(heads):
            mine = jnp.where(head_of == head, value, 1.0)
            v_ref[head, where, :] = jnp.where(real, mine, 0.0).astype(BF16)

    head_of = lax.broadcasted_iota(jnp.int32, (gsize, width), 1) // HD

    def copy2(slot, target):
        return pltpu.make_async_remote_copy(
            src_ref=send2.at[slot],
            dst_ref=recv2.at[me],
            send_sem=send2_sem.at[slot],
            recv_sem=recv2_sem.at[me],
            device_id={"stab": target},
            device_id_type=MESH,
        )

    def attend(step, _):
        group = groups - 1 - step
        first = pl.multiple_of(group * gsize, gsize)
        query = q_ref[pl.ds(first, gsize), :].astype(F32)
        above = jnp.zeros((gsize, width), F32)
        below = jnp.ones((gsize, width), F32)
        for head in range(heads):
            mine = jnp.where(head_of == head, query, 0.0).astype(BF16)
            scores = dot_t(mine, k_ref[...]) * HD ** (-0.5)
            peak = jnp.max(scores, axis=-1, keepdims=True)
            weights = jnp.exp(scores - peak).astype(BF16)
            both = dot(weights, v_ref[head])
            above = jnp.where(head_of == head, both, above)
            below = jnp.where(head_of == head, pltpu.roll(both, LANES, 1), below)
        mixed = above / below
        for index in range(GROUP):
            slot = group * GROUP + index
            send2[slot] = pack(mixed[index * rows : (index + 1) * rows])
        for index in range(GROUP - 1, -1, -1):
            slot = group * GROUP + index
            half = lax.div(slot + 1, 2)
            offset = jnp.where(lax.rem(slot, 2) == 1, half, -half)

            @pl.when(slot > 0)
            def _():
                copy2(slot, peer(offset)).start()

        return 0

    lax.fori_loop(0, groups, attend, 0)
    recv2[me] = send2[0]

    gain_rec = gain_rec_ref[...].astype(F32)
    for group in range(groups - 1, -1, -1):
        pieces, starts = [], []
        for slot in range(group * GROUP, (group + 1) * GROUP):
            item = peer(hop(slot))
            if slot:
                pltpu.make_async_remote_copy(
                    src_ref=send2.at[0],
                    dst_ref=recv2.at[item],
                    send_sem=send2_sem.at[slot],
                    recv_sem=recv2_sem.at[item],
                    device_id={"stab": peer(1)},
                    device_id_type=MESH,
                ).wait_recv()
            pieces.append(unpack(recv2[item]))
            starts.append(start_ref[item])
        mixed = jnp.concatenate(pieces, axis=0).astype(BF16)
        after = jnp.concatenate(starts, axis=0) + dot(mixed, wo_ref[...])
        rec_in = norm_rows(after, gain_rec).astype(BF16)
        decay = jax.nn.sigmoid(dot(rec_in, wd_ref[...]) + bias_ref[...])
        drive = (1.0 - decay) * dot(rec_in, wi_ref[...])
        for index in range(GROUP):
            item = peer(hop(group * GROUP + index))
            part = slice(index * rows, (index + 1) * rows)
            after_ref[item] = after[part]
            decay_ref[item] = decay[part]
            drive_ref[item] = drive[part]

    for shot in range(shots):
        state = drive_ref[shot * rounds]
        product = decay_ref[shot * rounds]
        for t in range(1, rounds):
            item = shot * rounds + t
            decay = decay_ref[item]
            state = decay * state + drive_ref[item]
            product = product * decay
            drive_ref[item] = state
            decay_ref[item] = product
        send3[shot, 0] = pack(product)
        send3[shot, 1] = pack(state)

    def copy3(offset):
        return pltpu.make_async_remote_copy(
            src_ref=send3,
            dst_ref=recv3.at[offset],
            send_sem=send3_sem.at[offset],
            recv_sem=recv3_sem.at[offset],
            device_id={"round": lax.rem(block + offset, blocks)},
            device_id_type=MESH,
        )

    for offset in range(1, blocks):

        @pl.when(block + offset < blocks)
        def _():
            copy3(offset).start()

    inc_ref[...] = jnp.zeros_like(inc_ref)
    for offset in range(blocks - 1, 0, -1):

        @pl.when(block >= offset)
        def _():
            copy3(offset).wait_recv()
            for shot in range(shots):
                product = unpack(recv3[offset, shot, 0])
                inc_ref[shot] = product * inc_ref[shot] + unpack(recv3[offset, shot, 1])

    gain_mlp = gain_mlp_ref[...].astype(F32)

    def finish(group, _):
        hiddens, afters = [], []
        for index in range(GROUP):
            item = group * GROUP + index
            shot = lax.div(item, rounds)
            hiddens.append(drive_ref[item] + decay_ref[item] * inc_ref[shot])
            afters.append(after_ref[item])
        hidden = jnp.concatenate(hiddens, axis=0).astype(BF16)
        after = jnp.concatenate(afters, axis=0) + dot(hidden, wr_ref[...])
        ffn_in = norm_rows(after, gain_mlp).astype(BF16)
        inner = (jax.nn.silu(dot(ffn_in, wg_ref[...])) * dot(ffn_in, wu_ref[...])).astype(BF16)
        states = after + dot(inner, wdown_ref[...])
        for index in range(GROUP):
            item = group * GROUP + index
            out_ref[lax.div(item, rounds), lax.rem(item, rounds)] = states[
                index * rows : index * rows + stabs
            ].astype(BF16)
        return 0

    lax.fori_loop(0, groups, finish, 0)

    for slot in range(1, parts):
        copy1(slot).wait_send()
        copy2(slot, peer(1)).wait_send()
    for offset in range(1, blocks):

        @pl.when(block + offset < blocks)
        def _():
            copy3(offset).wait_send()


def body(parts, blocks, *args):
    states_in, coord_table = args[0], args[3]
    shots, rounds, stabs, width = states_in.shape
    assert shots * rounds == parts
    rows = -(-stabs // 8) * 8
    flat = [arg.reshape(1, -1) if arg.ndim == 1 else arg for arg in args]
    message = (2 * rows, LANES)
    vmem = pl.BlockSpec(memory_space=pltpu.VMEM)
    dma = pltpu.SemaphoreType.DMA
    return pl.pallas_call(
        functools.partial(kernel, parts, blocks),
        out_shape=jax.ShapeDtypeStruct(states_in.shape, BF16),
        in_specs=[vmem] * len(flat),
        out_specs=vmem,
        scratch_shapes=[
            pltpu.VMEM((LANES, LANES), F32),
            pltpu.VMEM((parts, rows, width), F32),
            pltpu.VMEM((parts,) + message, BF16),
            pltpu.VMEM((parts,) + message, BF16),
            pltpu.VMEM((parts * rows, width), BF16),
            pltpu.VMEM((parts * rows, width), BF16),
            pltpu.VMEM((width // HD, parts * rows, width), BF16),
            pltpu.VMEM((parts,) + message, BF16),
            pltpu.VMEM((parts,) + message, BF16),
            pltpu.VMEM((parts, rows, width), F32),
            pltpu.VMEM((parts, rows, width), F32),
            pltpu.VMEM((parts, rows, width), F32),
            pltpu.VMEM((shots, 2) + message, BF16),
            pltpu.VMEM((blocks, shots, 2) + message, BF16),
            pltpu.VMEM((shots, rows, width), F32),
            dma((parts,)),
            dma((parts,)),
            dma((parts,)),
            dma((parts,)),
            dma((blocks,)),
            dma((blocks,)),
        ],
        compiler_params=pltpu.CompilerParams(
            collective_id=0, has_side_effects=True, vmem_limit_bytes=48 * 1024 * 1024
        ),
    )(*flat)


def solution(mesh):
    placed = (P("shot", "round", "stab", None), P("shot", "round", "stab"), P("round", "stab")) + (P(),) * 16
    return jax.shard_map(
        functools.partial(body, mesh.shape["stab"], mesh.shape["round"]),
        mesh=mesh,
        in_specs=placed,
        out_specs=P("shot", "round", "stab", None),
        check_vma=False,
    )
```

time: 273 us -> 78.7 us (0.29)
  waiting for transfers between devices: 173 us -> 0 us
  Pallas kernels: 0 us -> 63.2 us
  matrix products: 24 us -> 0 us
  starting transfers between devices: 15.7 us -> 0 us
  local copies, waits for them, and re-layouts: 29.9 us -> 14.4 us
  other arithmetic: 15.1 us -> 0 us
  between operations: 13.7 us -> 0.06 us
    all_gather x2 -> x0, waiting for transfers between devices: 140 us -> none  [the longest x1 83.2 us: body(): lax.all_gather(keys, 'stab', axis=2, tiled=True)]
    pallas_call x0 -> x1, Pallas kernels: none -> 63.2 us  [body(): pl.pallas_call(functools.partial(kernel, parts, blocks), out_shape=jax.Sh...]
    ppermute x7 -> x0, waiting for transfers between devices: 32.1 us -> none  [shifted(): lax.ppermute(value, axis, [(source, source + steps) for source in range(i...]
    dot_general x11 -> x0, matrix products: 24 us -> none  [the longest x1 9.95 us: softmax_step(): jnp.einsum('brhqk,brkhe->brqhe', expo.astype(jnp.bfloat16), value_piece,...]
    all_gather x2 -> x0, local copies, waits for them, and re-layouts: 17.8 us -> none  [the longest x1 8.89 us: body(): lax.all_gather(keys, 'stab', axis=2, tiled=True)]
    ppermute x7 -> x0, starting transfers between devices: 15.7 us -> none  [shifted(): lax.ppermute(value, axis, [(source, source + steps) for source in range(i...]
    dynamic_update_slice x8 -> x0, other arithmetic: 5.52 us -> none  [body(): lax.scan(advance, (zero_state, unit_state), (jnp.moveaxis(decay, 1, 0), j...]
    unnamed x24 -> x29, local copies, waits for them, and re-layouts: 5.53 us -> 10.9 us
  transfers between devices with their start and end apart: 9 -> 0, of which waited for: 9 -> 0; matrix products, arithmetic and copies ran while one was open for 7% -> 0% of each run, Pallas kernels for 0% -> 0%
where the time goes in v1:
time: 78.7 us; the launch traced here: 77.6 us
  Pallas kernels  63.2 us (80%)
  local copies, waits for them, and re-layouts  14.4 us (18%)
    pallas_call x1, Pallas kernels, body(): pl.pallas_call(functools.partial(kernel, parts, blocks), out_shape=jax.Sh...  63.2 us
    unnamed x29, local copies, waits for them, and re-layouts  10.9 us
    reshape x4, local copies, waits for them, and re-layouts, body(): flat = [arg.reshape(1, -1) if arg.ndim == 1 else arg for arg in args]  2.69 us

profile of v1, /device:TPU:24, one launch (start us, length us, event | category | flops | bytes accessed | tf_op | source)
XLA Modules:
  0.0 77.6 jit_solution(563859310924228935)
XLA Ops:
  0.0 0.0 copy-start
  0.0 0.7 reshape.15.flip_ref
  0.7 0.7 reshape.16.gain_attn_ref
  1.4 0.7 reshape.17.gain_rec_ref
  2.0 0.7 reshape.19.gain_mlp_ref
  2.7 0.0 copy-start.4
  2.7 1.1 %copy.20.states_ref = bf16[2,8,39,256]{3,2,1,0:T(8,128)(2,1)S(1)} copy(bf16[2,8,39,256]{3,1,2,0:T(8,128)(2,1)} %param.19) | data formatting | bytes 638976 | tf_op args[0]
  3.8 0.0 copy-done
  3.8 0.0 copy-done.4
  3.8 0.0 copy-done.13
  3.8 0.0 copy-start.1
  3.8 1.0 %copy-done.1 = bf16[256,1024]{1,0:T(8,128)(2,1)S(1)} copy-done((bf16[256,1024]{1,0:T(8,128)(2,1)S(1)}, bf16[256,1024]{1,0:T(8,128)(2,1)}, u32[]{:S(2)}) %copy-start.1) | copy-done | bytes 524312
  4.8 1.0 %copy-done.2 = bf16[1024,256]{1,0:T(8,128)(2,1)S(1)} copy-done((bf16[1024,256]{1,0:T(8,128)(2,1)S(1)}, bf16[1024,256]{1,0:T(8,128)(2,1)}, u32[]{:S(2)}) %copy-start.2) | copy-done | bytes 524312
  5.9 1.0 %copy-done.3 = bf16[625,256]{1,0:T(8,128)(2,1)S(1)} copy-done((bf16[625,256]{1,0:T(8,128)(2,1)S(1)}, bf16[625,256]{1,0:T(8,128)(2,1)}, u32[]{:S(2)}) %copy-start.3) | copy-done | bytes 320024
  6.9 0.9 %copy-done.5 = bf16[256,256]{1,0:T(8,128)(2,1)S(1)} copy-done((bf16[256,256]{1,0:T(8,128)(2,1)S(1)}, bf16[256,256]{1,0:T(8,128)(2,1)}, u32[]{:S(2)}) %copy-start.5) | copy-done | bytes 131096
  7.8 0.9 %copy-done.6 = bf16[256,256]{1,0:T(8,128)(2,1)S(1)} copy-done((bf16[256,256]{1,0:T(8,128)(2,1)S(1)}, bf16[256,256]{1,0:T(8,128)(2,1)}, u32[]{:S(2)}) %copy-start.6) | copy-done | bytes 131096
  8.7 0.9 %copy-done.7 = bf16[256,256]{1,0:T(8,128)(2,1)S(1)} copy-done((bf16[256,256]{1,0:T(8,128)(2,1)S(1)}, bf16[256,256]{1,0:T(8,128)(2,1)}, u32[]{:S(2)}) %copy-start.7) | copy-done | bytes 131096
  9.6 0.9 %copy-done.8 = bf16[256,256]{1,0:T(8,128)(2,1)S(1)} copy-done((bf16[256,256]{1,0:T(8,128)(2,1)S(1)}, bf16[256,256]{1,0:T(8,128)(2,1)}, u32[]{:S(2)}) %copy-start.8) | copy-done | bytes 131096
  10.5 0.9 %copy-done.9 = bf16[256,256]{1,0:T(8,128)(2,1)S(1)} copy-done((bf16[256,256]{1,0:T(8,128)(2,1)S(1)}, bf16[256,256]{1,0:T(8,128)(2,1)}, u32[]{:S(2)}) %copy-start.9) | copy-done | bytes 131096
  11.4 0.9 %copy-done.10 = bf16[256,256]{1,0:T(8,128)(2,1)S(1)} copy-done((bf16[256,256]{1,0:T(8,128)(2,1)S(1)}, bf16[256,256]{1,0:T(8,128)(2,1)}, u32[]{:S(2)}) %copy-start.10) | copy-done | bytes 131096
  12.3 0.7 copy-done.11
  13.0 0.7 copy-done.12
  13.7 63.2 %shard_map.181 = bf16[2,8,39,256]{3,2,1,0:T(8,128)(2,1)S(1)} custom-call(bf16[2,8,39,256]{3,2,1,0:T(8,128)(2,1)S(1)} %copy.20.states_ref, s32[2,8,39]{2,1,0:T(8,128)S(1)} %copy-done.11, s32[8,39]{1,0:T(8,128)S(1)} %copy-done.12, bf16[625,256]{1,0:T(8,128)(2,1)S(1)} %copy-done.3, bf16[1,256]{1,0:T(2,128)(2,1)S(1)} %reshape.15.flip_ref, ...), custom_call_target="tpu_custom_call" | custom-call | tf_op jit(solution)/shard_map/pallas_call | solution.py:335
  76.9 0.8 %copy.21 = bf16[2,8,39,256]{3,1,2,0:T(8,128)(2,1)} copy(bf16[2,8,39,256]{3,2,1,0:T(8,128)(2,1)S(1)} %shard_map.181) | data formatting | bytes 638976 | tf_op jit(solution)/shard_map/pallas_call | solution.py:335
  (11 shorter events, 0.0 us)
Async XLA Ops:
  0.0 3.8 %copy-start = (bf16[256,1024]{1,0:T(8,128)(2,1)S(1)}, bf16[256,1024]{1,0:T(8,128)(2,1)}, u32[]{:S(2)}) copy-start(bf16[256,1024]{1,0:T(8,128)(2,1)} %wg_ref.1) | copy-start | bytes 1572868
  2.7 1.1 %copy-start.4 = (bf16[256,256]{1,0:T(8,128)(2,1)S(1)}, bf16[256,256]{1,0:T(8,128)(2,1)}, u32[]{:S(2)}) copy-start(bf16[256,256]{1,0:T(8,128)(2,1)} %wq_ref.1) | copy-start | bytes 393220
  2.7 1.1 %copy-start.13 = (f32[256]{0:T(256)S(1)}, f32[256]{0:T(256)}, u32[]{:S(2)}) copy-start(f32[256]{0:T(256)} %param.31) | copy-start | bytes 3076
  3.8 1.0 %copy-start.1 = (bf16[256,1024]{1,0:T(8,128)(2,1)S(1)}, bf16[256,1024]{1,0:T(8,128)(2,1)}, u32[]{:S(2)}) copy-start(bf16[256,1024]{1,0:T(8,128)(2,1)} %wu_ref.1) | copy-start | bytes 1572868
  4.8 1.0 %copy-start.2 = (bf16[1024,256]{1,0:T(8,128)(2,1)S(1)}, bf16[1024,256]{1,0:T(8,128)(2,1)}, u32[]{:S(2)}) copy-start(bf16[1024,256]{1,0:T(8,128)(2,1)} %wdown_ref.1) | copy-start | bytes 1572868
  5.9 1.0 %copy-start.3 = (bf16[625,256]{1,0:T(8,128)(2,1)S(1)}, bf16[625,256]{1,0:T(8,128)(2,1)}, u32[]{:S(2)}) copy-start(bf16[625,256]{1,0:T(8,128)(2,1)} %table_ref.1) | copy-start | bytes 960004
  6.9 0.9 %copy-start.5 = (bf16[256,256]{1,0:T(8,128)(2,1)S(1)}, bf16[256,256]{1,0:T(8,128)(2,1)}, u32[]{:S(2)}) copy-start(bf16[256,256]{1,0:T(8,128)(2,1)} %wk_ref.1) | copy-start | bytes 393220
  7.8 0.9 %copy-start.6 = (bf16[256,256]{1,0:T(8,128)(2,1)S(1)}, bf16[256,256]{1,0:T(8,128)(2,1)}, u32[]{:S(2)}) copy-start(bf16[256,256]{1,0:T(8,128)(2,1)} %wv_ref.1) | copy-start | bytes 393220
  8.7 0.9 %copy-start.7 = (bf16[256,256]{1,0:T(8,128)(2,1)S(1)}, bf16[256,256]{1,0:T(8,128)(2,1)}, u32[]{:S(2)}) copy-start(bf16[256,256]{1,0:T(8,128)(2,1)} %wo_ref.1) | copy-start | bytes 393220
  9.6 0.9 %copy-start.8 = (bf16[256,256]{1,0:T(8,128)(2,1)S(1)}, bf16[256,256]{1,0:T(8,128)(2,1)}, u32[]{:S(2)}) copy-start(bf16[256,256]{1,0:T(8,128)(2,1)} %wd_ref.1) | copy-start | bytes 393220
  10.5 0.9 %copy-start.9 = (bf16[256,256]{1,0:T(8,128)(2,1)S(1)}, bf16[256,256]{1,0:T(8,128)(2,1)}, u32[]{:S(2)}) copy-start(bf16[256,256]{1,0:T(8,128)(2,1)} %wi_ref.1) | copy-start | bytes 393220
  11.4 0.9 %copy-start.10 = (bf16[256,256]{1,0:T(8,128)(2,1)S(1)}, bf16[256,256]{1,0:T(8,128)(2,1)}, u32[]{:S(2)}) copy-start(bf16[256,256]{1,0:T(8,128)(2,1)} %wr_ref.1) | copy-start | bytes 393220
  12.3 0.7 copy-start.11
  13.0 0.7 copy-start.12

commit v2 on v1

--- a/solution.py
+++ b/solution.py
@@ -10,6 +10,7 @@
 HD = 32
 LANES = 128
 GROUP = 4
+INPUTS = 19
 MESH = pl.DeviceIdType.MESH
 F32 = jnp.float32
 BF16 = jnp.bfloat16
@@ -26,6 +27,10 @@
 def norm_rows(values, gain):
     scale = lax.rsqrt(jnp.mean(values * values, axis=-1, keepdims=True) + 1e-05)
     return values * scale * gain
+
+
+def row(ref):
+    return ref[...].astype(F32).reshape(1, -1)
 
 
 def pack(rows):
@@ -42,29 +47,20 @@
     return (slot + 1) // 2 if slot % 2 else -(slot // 2)
 
 
-def kernel(
+def kernel(parts, blocks, *refs):
+    sources, refs = refs[:INPUTS], refs[INPUTS:]
+    out_ref, refs = refs[0], refs[1:]
+    operands, refs = refs[:INPUTS], refs[INPUTS:]
+    run(parts, blocks, sources, out_ref, operands, *refs)
+
+
+def run(
     parts,
     blocks,
-    states_ref,
-    bits_ref,
-    coords_ref,
-    table_ref,
-    flip_ref,
-    gain_attn_ref,
-    wq_ref,
-    wk_ref,
-    wv_ref,
-    wo_ref,
-    gain_rec_ref,
-    wd_ref,
-    bias_ref,
-    wi_ref,
-    wr_ref,
-    gain_mlp_ref,
-    wg_ref,
-    wu_ref,
-    wdown_ref,
+    sources,
     out_ref,
+    operands,
+    wide_ref,
     small_ref,
     start_ref,
     send1,
@@ -86,8 +82,12 @@
     recv2_sem,
     send3_sem,
     recv3_sem,
+    load_sem,
 ):
-    shots, rounds, stabs, width = states_ref.shape
+    (states_ref, bits_ref, coords_ref, table_ref, flip_ref, gain_attn_ref, wq_ref, wk_ref, wv_ref, wo_ref) = operands[:10]
+    (gain_rec_ref, wd_ref, bias_ref, wi_ref, wr_ref, gain_mlp_ref, wg_ref, wu_ref, wdown_ref) = operands[10:]
+    shots, rounds, stabs = bits_ref.shape
+    width = states_ref.shape[1]
     rows = start_ref.shape[1]
     coord_rows = table_ref.shape[0]
     heads = width // HD
@@ -100,6 +100,9 @@
     def peer(offset):
         return lax.rem(me + (offset + parts), parts)
 
+    def load(index):
+        return pltpu.make_async_copy(sources[index], operands[index], load_sem.at[index])
+
     barrier = pltpu.get_barrier_semaphore()
     for offset in range(1, parts):
         pl.semaphore_signal(barrier, inc=1, device_id={"stab": peer(offset)}, device_id_type=MESH)
@@ -108,6 +111,13 @@
             barrier, inc=1, device_id={"round": lax.rem(block + offset, blocks)}, device_id_type=MESH
         )
 
+    for index in range(INPUTS):
+        load(index).start()
+
+    for index in range(6):
+        load(index).wait()
+    for half in range(2):
+        wide_ref[half] = states_ref[:, half * LANES : (half + 1) * LANES].astype(F32)
     small_ref[...] = jnp.zeros_like(small_ref)
     small_ref[0:rounds, 0:stabs] = coords_ref[...].astype(F32)
     for shot in range(shots):
@@ -116,8 +126,8 @@
     turned = jnp.transpose(small_ref[...])
     small_ref[...] = turned
     small_ref[stabs : stabs + 1, :] = small_ref[stabs - 1 : stabs, :]
-    flip = flip_ref[...].astype(F32)
-    gain_attn = gain_attn_ref[...].astype(F32)
+    flip = row(flip_ref)
+    gain_attn = row(gain_attn_ref)
     spot = lax.broadcasted_iota(jnp.int32, (rows, coord_rows), 1).astype(F32)
     for pair in range(rounds // 2):
         picks = []
@@ -129,7 +139,8 @@
             for shot in range(shots):
                 item = shot * rounds + t
                 lane = rounds * (1 + shot) + t
-                own = states_ref[shot, t].astype(F32)
+                where = pl.ds(shot * stabs * rounds + t, stabs, stride=rounds)
+                own = jnp.concatenate([wide_ref[0, where, :], wide_ref[1, where, :]], axis=1)
                 start_ref[item, 0:stabs, :] = own
                 start_ref[item, stabs : stabs + 1, :] = own[stabs - 1 : stabs, :]
                 sign = 2.0 * small_ref[0:rows, lane : lane + 1] - 1.0
@@ -155,6 +166,8 @@
         copy1(slot).start()
     recv1[0] = send1[me]
 
+    for index in range(6, INPUTS):
+        load(index).wait()
     real = lax.rem(lax.broadcasted_iota(jnp.int32, (gsize, 1), 0), rows) < stabs
     for group in range(groups):
         pieces = []
@@ -223,7 +236,7 @@
     lax.fori_loop(0, groups, attend, 0)
     recv2[me] = send2[0]
 
-    gain_rec = gain_rec_ref[...].astype(F32)
+    gain_rec = row(gain_rec_ref)
     for group in range(groups - 1, -1, -1):
         pieces, starts = [], []
         for slot in range(group * GROUP, (group + 1) * GROUP):
@@ -242,7 +255,7 @@
         mixed = jnp.concatenate(pieces, axis=0).astype(BF16)
         after = jnp.concatenate(starts, axis=0) + dot(mixed, wo_ref[...])
         rec_in = norm_rows(after, gain_rec).astype(BF16)
-        decay = jax.nn.sigmoid(dot(rec_in, wd_ref[...]) + bias_ref[...])
+        decay = jax.nn.sigmoid(dot(rec_in, wd_ref[...]) + row(bias_ref))
         drive = (1.0 - decay) * dot(rec_in, wi_ref[...])
         for index in range(GROUP):
             item = peer(hop(group * GROUP + index))
@@ -290,7 +303,7 @@
                 product = unpack(recv3[offset, shot, 0])
                 inc_ref[shot] = product * inc_ref[shot] + unpack(recv3[offset, shot, 1])
 
-    gain_mlp = gain_mlp_ref[...].astype(F32)
+    gain_mlp = row(gain_mlp_ref)
 
     def finish(group, _):
         hiddens, afters = [], []
@@ -306,12 +319,16 @@
         states = after + dot(inner, wdown_ref[...])
         for index in range(GROUP):
             item = group * GROUP + index
-            out_ref[lax.div(item, rounds), lax.rem(item, rounds)] = states[
-                index * rows : index * rows + stabs
-            ].astype(BF16)
+            first = lax.div(item, rounds) * (stabs * rounds) + lax.rem(item, rounds)
+            for half in range(2):
+                wide_ref[half, pl.ds(first, stabs, stride=rounds), :] = states[
+                    index * rows : index * rows + stabs, half * LANES : (half + 1) * LANES
+                ]
         return 0
 
     lax.fori_loop(0, groups, finish, 0)
+    for half in range(2):
+        out_ref[:, half * LANES : (half + 1) * LANES] = wide_ref[half].astype(BF16)
 
     for slot in range(1, parts):
         copy1(slot).wait_send()
@@ -324,20 +341,23 @@
 
 
 def body(parts, blocks, *args):
-    states_in, coord_table = args[0], args[3]
+    states_in = args[0]
     shots, rounds, stabs, width = states_in.shape
     assert shots * rounds == parts
+    assert len(args) == INPUTS
     rows = -(-stabs // 8) * 8
-    flat = [arg.reshape(1, -1) if arg.ndim == 1 else arg for arg in args]
+    flat = (jnp.transpose(states_in, (0, 2, 1, 3)).reshape(-1, width),) + args[1:]
     message = (2 * rows, LANES)
     vmem = pl.BlockSpec(memory_space=pltpu.VMEM)
     dma = pltpu.SemaphoreType.DMA
-    return pl.pallas_call(
+    result = pl.pallas_call(
         functools.partial(kernel, parts, blocks),
-        out_shape=jax.ShapeDtypeStruct(states_in.shape, BF16),
-        in_specs=[vmem] * len(flat),
+        out_shape=jax.ShapeDtypeStruct(flat[0].shape, BF16),
+        in_specs=[pl.BlockSpec(memory_space=pltpu.HBM)] * len(flat),
         out_specs=vmem,
-        scratch_shapes=[
+        scratch_shapes=[pltpu.VMEM(arg.shape, arg.dtype) for arg in flat]
+        + [
+            pltpu.VMEM((2, flat[0].shape[0], LANES), F32),
             pltpu.VMEM((LANES, LANES), F32),
             pltpu.VMEM((parts, rows, width), F32),
             pltpu.VMEM((parts,) + message, BF16),
@@ -359,11 +379,13 @@
             dma((parts,)),
             dma((blocks,)),
             dma((blocks,)),
+            dma((INPUTS,)),
         ],
         compiler_params=pltpu.CompilerParams(
-            collective_id=0, has_side_effects=True, vmem_limit_bytes=48 * 1024 * 1024
+            collective_id=0, has_side_effects=True, vmem_limit_bytes=58 * 1024 * 1024
         ),
     )(*flat)
+    return jnp.transpose(result.reshape(shots, stabs, rounds, width), (0, 2, 1, 3))
 
 
 def solution(mesh):

time: 78.7 us -> 66.5 us (0.84)
  local copies, waits for them, and re-layouts: 14.4 us -> 1.71 us
  Pallas kernels: 63.2 us -> 64.1 us
    unnamed x29 -> x1, local copies, waits for them, and re-layouts: 10.9 us -> 1.71 us
    reshape x4 -> x0, local copies, waits for them, and re-layouts: 2.69 us -> none  [body(): flat = [arg.reshape(1, -1) if arg.ndim == 1 else arg for arg in args]]
    pallas_call x1, Pallas kernels: 63.2 us -> 64.1 us  [body(): pl.pallas_call(functools.partial(kernel, parts, blocks), out_shape=jax.Sh...]
where the time goes in v2:
time: 66.5 us; the launch traced here: 65.8 us
  Pallas kernels  64.1 us (96%)
  local copies, waits for them, and re-layouts  1.71 us (3%)
    pallas_call x1, Pallas kernels, body(): pl.pallas_call(functools.partial(kernel, parts, blocks), out_shape=jax.Sh...  64.1 us
    unnamed x1, local copies, waits for them, and re-layouts  1.71 us

profile of v2, /device:TPU:24, one launch (start us, length us, event | category | flops | bytes accessed | tf_op | source)
XLA Modules:
  0.0 65.8 jit_solution(17102926031549657826)
XLA Ops:
  0.0 64.1 %shard_map.181 = bf16[624,256]{1,0:T(8,128)(2,1)} custom-call(bf16[624,256]{1,0:T(8,128)(2,1)} %bitcast.7, s32[2,8,39]{2,1,0:T(8,128)} %refs_1_.1, s32[8,39]{1,0:T(8,128)} %refs_2_.1, bf16[625,256]{1,0:T(8,128)(2,1)} %refs_3_.1, bf16[256]{0:T(256)(128)(2,1)} %refs_4_.1, bf16[256]{0:T(256)(128)(2,1)} %refs_5_.1, bf16[256,256]{1,0:T(8,128)(2,1)} %refs_6_.1, ...), custom_call_target="tpu_custom_call" | custom-call | tf_op jit(solution)/shard_map/pallas_call | solution.py:353
  64.1 1.7 %copy.21 = bf16[2,8,39,256]{3,1,2,0:T(8,128)(2,1)} copy(bf16[2,8,39,256]{3,1,2,0:T(8,128)(2,1)} %bitcast.6) | data formatting | bytes 638976

commit v3 on v2

--- a/solution.py
+++ b/solution.py
@@ -1,4 +1,5 @@
 import functools
+import math
 
 import jax
 import jax.numpy as jnp
@@ -11,6 +12,7 @@
 LANES = 128
 GROUP = 4
 INPUTS = 19
+QUERIES = 256
 MESH = pl.DeviceIdType.MESH
 F32 = jnp.float32
 BF16 = jnp.bfloat16
@@ -68,6 +70,10 @@
     q_ref,
     k_ref,
     v_ref,
+    n_ref,
+    turned_ref,
+    across_ref,
+    mixed_ref,
     send2,
     recv2,
     after_ref,
@@ -75,6 +81,8 @@
     drive_ref,
     send3,
     recv3,
+    send4,
+    recv4,
     inc_ref,
     send1_sem,
     recv1_sem,
@@ -82,6 +90,8 @@
     recv2_sem,
     send3_sem,
     recv3_sem,
+    send4_sem,
+    recv4_sem,
     load_sem,
 ):
     (states_ref, bits_ref, coords_ref, table_ref, flip_ref, gain_attn_ref, wq_ref, wk_ref, wv_ref, wo_ref) = operands[:10]
@@ -168,7 +178,7 @@
 
     for index in range(6, INPUTS):
         load(index).wait()
-    real = lax.rem(lax.broadcasted_iota(jnp.int32, (gsize, 1), 0), rows) < stabs
+    turned_ref[...] = jnp.transpose(wv_ref[...].astype(F32)).astype(BF16)
     for group in range(groups):
         pieces = []
         for slot in range(group * GROUP, (group + 1) * GROUP):
@@ -186,13 +196,13 @@
         where = slice(group * gsize, (group + 1) * gsize)
         q_ref[where, :] = dot(normed, wq_ref[...]).astype(BF16)
         k_ref[where, :] = dot(normed, wk_ref[...]).astype(BF16)
-        value = dot(normed, wv_ref[...])
-        head_of = lax.broadcasted_iota(jnp.int32, (gsize, width), 1) // HD
-        for head in range(heads):
-            mine = jnp.where(head_of == head, value, 1.0)
-            v_ref[head, where, :] = jnp.where(real, mine, 0.0).astype(BF16)
-
-    head_of = lax.broadcasted_iota(jnp.int32, (gsize, width), 1) // HD
+        n_ref[where, :] = normed
+    real = lax.rem(lax.broadcasted_iota(jnp.int32, (1, keys), 1), rows) < stabs
+    values = jnp.where(real, dot_t(turned_ref[...], n_ref[...]), 0.0)
+    ones = jnp.where(real, jnp.ones((v_ref.shape[1] - HD, keys), F32), 0.0).astype(BF16)
+    for head in range(heads):
+        v_ref[head, 0:HD, :] = values[head * HD : (head + 1) * HD].astype(BF16)
+        v_ref[head, HD:, :] = ones
 
     def copy2(slot, target):
         return pltpu.make_async_remote_copy(
@@ -204,36 +214,26 @@
             device_id_type=MESH,
         )
 
-    def attend(step, _):
-        group = groups - 1 - step
-        first = pl.multiple_of(group * gsize, gsize)
-        query = q_ref[pl.ds(first, gsize), :].astype(F32)
-        above = jnp.zeros((gsize, width), F32)
-        below = jnp.ones((gsize, width), F32)
+    scale = HD ** (-0.5) * math.log2(math.e)
+    done = parts
+    for last in range(keys, 0, -QUERIES):
+        first = max(last - QUERIES, 0)
+        count = last - first
+        query = q_ref[first:last, :].astype(F32)
+        head_of = lax.broadcasted_iota(jnp.int32, (count, width), 1) // HD
         for head in range(heads):
             mine = jnp.where(head_of == head, query, 0.0).astype(BF16)
-            scores = dot_t(mine, k_ref[...]) * HD ** (-0.5)
-            peak = jnp.max(scores, axis=-1, keepdims=True)
-            weights = jnp.exp(scores - peak).astype(BF16)
-            both = dot(weights, v_ref[head])
-            above = jnp.where(head_of == head, both, above)
-            below = jnp.where(head_of == head, pltpu.roll(both, LANES, 1), below)
-        mixed = above / below
-        for index in range(GROUP):
-            slot = group * GROUP + index
-            send2[slot] = pack(mixed[index * rows : (index + 1) * rows])
-        for index in range(GROUP - 1, -1, -1):
-            slot = group * GROUP + index
-            half = lax.div(slot + 1, 2)
-            offset = jnp.where(lax.rem(slot, 2) == 1, half, -half)
-
-            @pl.when(slot > 0)
-            def _():
-                copy2(slot, peer(offset)).start()
-
-        return 0
-
-    lax.fori_loop(0, groups, attend, 0)
+            scores = dot_t(k_ref[...], mine)
+            peak = jnp.max(scores, axis=0, keepdims=True)
+            weights = jnp.exp2((scores - peak) * scale).astype(BF16)
+            both = dot(v_ref[head], weights)
+            across_ref[head * HD : (head + 1) * HD, 0:count] = both[:HD] / both[HD : HD + 1]
+        mixed_ref[first:last, :] = jnp.transpose(across_ref[:, 0:count])
+        while done > 0 and (done - 1) * rows >= first:
+            done -= 1
+            send2[done] = pack(mixed_ref[done * rows : (done + 1) * rows, :])
+            if done:
+                copy2(done, peer(hop(done))).start()
     recv2[me] = send2[0]
 
     gain_rec = row(gain_rec_ref)
@@ -274,34 +274,84 @@
             product = product * decay
             drive_ref[item] = state
             decay_ref[item] = product
-        send3[shot, 0] = pack(product)
-        send3[shot, 1] = pack(state)
-
-    def copy3(offset):
+        for half in range(2):
+            part = slice(half * LANES, (half + 1) * LANES)
+            send3[2 * shot + half] = jnp.concatenate([product[:, part], state[:, part]], axis=0).astype(BF16)
+
+    chunks = 2 * shots
+    step = blocks // chunks
+    shift = lax.rem(lax.axis_index("shot"), step)
+    my_chunk = lax.div(block, step)
+    owner = lax.rem(block, step) == shift
+
+    def copy3(chunk):
         return pltpu.make_async_remote_copy(
-            src_ref=send3,
-            dst_ref=recv3.at[offset],
-            send_sem=send3_sem.at[offset],
-            recv_sem=recv3_sem.at[offset],
-            device_id={"round": lax.rem(block + offset, blocks)},
+            src_ref=send3.at[chunk],
+            dst_ref=recv3.at[block],
+            send_sem=send3_sem.at[chunk],
+            recv_sem=recv3_sem.at[block],
+            device_id={"round": chunk * step + shift},
             device_id_type=MESH,
         )
 
-    for offset in range(1, blocks):
-
-        @pl.when(block + offset < blocks)
+    def copy4(target):
+        return pltpu.make_async_remote_copy(
+            src_ref=send4.at[target],
+            dst_ref=recv4.at[my_chunk],
+            send_sem=send4_sem.at[target],
+            recv_sem=recv4_sem.at[my_chunk],
+            device_id={"round": target},
+            device_id_type=MESH,
+        )
+
+    for chunk in range(chunks):
+
+        @pl.when(block != chunk * step + shift)
         def _():
-            copy3(offset).start()
-
-    inc_ref[...] = jnp.zeros_like(inc_ref)
-    for offset in range(blocks - 1, 0, -1):
-
-        @pl.when(block >= offset)
+            copy3(chunk).start()
+
+        @pl.when(block == chunk * step + shift)
         def _():
-            copy3(offset).wait_recv()
-            for shot in range(shots):
-                product = unpack(recv3[offset, shot, 0])
-                inc_ref[shot] = product * inc_ref[shot] + unpack(recv3[offset, shot, 1])
+            recv3[block] = send3[chunk]
+
+    @pl.when(owner)
+    def _():
+        entering = jnp.zeros((rows, LANES), F32)
+        below = jnp.zeros((send4.shape[1] - rows, LANES), F32)
+        for source in range(blocks):
+            send4[source] = jnp.concatenate([entering, below], axis=0).astype(BF16)
+
+            @pl.when(block != source)
+            def _():
+                copy4(source).start()
+                pltpu.make_async_remote_copy(
+                    src_ref=send3.at[0],
+                    dst_ref=recv3.at[source],
+                    send_sem=send3_sem.at[0],
+                    recv_sem=recv3_sem.at[source],
+                    device_id={"round": source},
+                    device_id_type=MESH,
+                ).wait_recv()
+
+            wide = recv3[source].astype(F32)
+            entering = wide[:rows] * entering + wide[rows:]
+        recv4[my_chunk] = send4[block]
+
+    for chunk in range(chunks):
+
+        @pl.when(block != chunk * step + shift)
+        def _():
+            pltpu.make_async_remote_copy(
+                src_ref=send4.at[0],
+                dst_ref=recv4.at[chunk],
+                send_sem=send4_sem.at[0],
+                recv_sem=recv4_sem.at[chunk],
+                device_id={"round": chunk * step + shift},
+                device_id_type=MESH,
+            ).wait_recv()
+
+        part = slice((chunk % 2) * LANES, (chunk % 2 + 1) * LANES)
+        inc_ref[chunk // 2, :, part] = recv4[chunk].astype(F32)[:rows]
 
     gain_mlp = row(gain_mlp_ref)
 
@@ -333,11 +383,17 @@
     for slot in range(1, parts):
         copy1(slot).wait_send()
         copy2(slot, peer(1)).wait_send()
-    for offset in range(1, blocks):
-
-        @pl.when(block + offset < blocks)
+    for chunk in range(chunks):
+
+        @pl.when(block != chunk * step + shift)
         def _():
-            copy3(offset).wait_send()
+            copy3(chunk).wait_send()
+
+    for target in range(blocks):
+
+        @pl.when(owner & (block != target))
+        def _():
+            copy4(target).wait_send()
 
 
 def body(parts, blocks, *args):
@@ -352,7 +408,7 @@
     dma = pltpu.SemaphoreType.DMA
     result = pl.pallas_call(
         functools.partial(kernel, parts, blocks),
-        out_shape=jax.ShapeDtypeStruct(flat[0].shape, BF16),
+        out_shape=pltpu.VMEM(flat[0].shape, BF16),
         in_specs=[pl.BlockSpec(memory_space=pltpu.HBM)] * len(flat),
         out_specs=vmem,
         scratch_shapes=[pltpu.VMEM(arg.shape, arg.dtype) for arg in flat]
@@ -364,21 +420,29 @@
             pltpu.VMEM((parts,) + message, BF16),
             pltpu.VMEM((parts * rows, width), BF16),
             pltpu.VMEM((parts * rows, width), BF16),
-            pltpu.VMEM((width // HD, parts * rows, width), BF16),
+            pltpu.VMEM((width // HD, HD + 16, parts * rows), BF16),
+            pltpu.VMEM((parts * rows, width), BF16),
+            pltpu.VMEM((width, width), BF16),
+            pltpu.VMEM((width, QUERIES), F32),
+            pltpu.VMEM((parts * rows, width), F32),
             pltpu.VMEM((parts,) + message, BF16),
             pltpu.VMEM((parts,) + message, BF16),
             pltpu.VMEM((parts, rows, width), F32),
             pltpu.VMEM((parts, rows, width), F32),
             pltpu.VMEM((parts, rows, width), F32),
-            pltpu.VMEM((shots, 2) + message, BF16),
-            pltpu.VMEM((blocks, shots, 2) + message, BF16),
+            pltpu.VMEM((2 * shots,) + message, BF16),
+            pltpu.VMEM((blocks,) + message, BF16),
+            pltpu.VMEM((blocks, -(-rows // 16) * 16, LANES), BF16),
+            pltpu.VMEM((2 * shots, -(-rows // 16) * 16, LANES), BF16),
             pltpu.VMEM((shots, rows, width), F32),
             dma((parts,)),
             dma((parts,)),
             dma((parts,)),
             dma((parts,)),
+            dma((2 * shots,)),
             dma((blocks,)),
             dma((blocks,)),
+            dma((2 * shots,)),
             dma((INPUTS,)),
         ],
         compiler_params=pltpu.CompilerParams(

time: 66.5 us -> 63.4 us (0.953)
  Pallas kernels: 64.1 us -> 62.5 us
  local copies, waits for them, and re-layouts: 1.71 us -> 0.72 us
    pallas_call x1, Pallas kernels: 64.1 us -> 62.5 us  [body(): pl.pallas_call(functools.partial(kernel, parts, blocks), out_shape=pltpu....]
    unnamed x1, local copies, waits for them, and re-layouts: 1.71 us -> 0.72 us
where the time goes in v3:
time: 63.4 us; the launch traced here: 63.2 us
  Pallas kernels  62.5 us (99%)
  local copies, waits for them, and re-layouts  0.72 us (1%)
    pallas_call x1, Pallas kernels, body(): pl.pallas_call(functools.partial(kernel, parts, blocks), out_shape=pltpu....  62.5 us

profile of v3, /device:TPU:24, one launch (start us, length us, event | category | flops | bytes accessed | tf_op | source)
XLA Modules:
  0.0 63.2 jit_solution(129504716371013015)
XLA Ops:
  0.0 62.5 %shard_map.181 = bf16[624,256]{1,0:T(8,128)(2,1)S(1)} custom-call(bf16[624,256]{1,0:T(8,128)(2,1)} %bitcast.7, s32[2,8,39]{2,1,0:T(8,128)} %refs_1_.1, s32[8,39]{1,0:T(8,128)} %refs_2_.1, bf16[625,256]{1,0:T(8,128)(2,1)} %refs_3_.1, bf16[256]{0:T(256)(128)(2,1)} %refs_4_.1, bf16[256]{0:T(256)(128)(2,1)} %refs_5_.1, bf16[256,256]{1,0:T(8,128)(2,1)} %refs_6_.1, ...), custom_call_target="tpu_custom_call" | custom-call | tf_op jit(solution)/shard_map/pallas_call | solution.py:409
  62.5 0.7 %copy.21 = bf16[2,8,39,256]{3,1,2,0:T(8,128)(2,1)} copy(bf16[2,8,39,256]{3,1,2,0:T(8,128)(2,1)S(1)} %bitcast.6) | data formatting | bytes 638976

commit v4 on v3

--- a/solution.py
+++ b/solution.py
@@ -12,7 +12,10 @@
 LANES = 128
 GROUP = 4
 INPUTS = 19
-QUERIES = 256
+FINISH = 8
+BASE = 32
+COUNTS = (128, 256, 256)
+ARRIVALS = ((0, 1, 2, 3), (4, 5, 6, 7), (8, 9, 10, 11), (12, 13), (14, 15))
 MESH = pl.DeviceIdType.MESH
 F32 = jnp.float32
 BF16 = jnp.bfloat16
@@ -64,6 +67,7 @@
     operands,
     wide_ref,
     small_ref,
+    loose_ref,
     start_ref,
     send1,
     recv1,
@@ -124,39 +128,24 @@
     for index in range(INPUTS):
         load(index).start()
 
-    for index in range(6):
+    small_ref[...] = jnp.zeros_like(small_ref)
+    for index in range(3):
         load(index).wait()
     for half in range(2):
         wide_ref[half] = states_ref[:, half * LANES : (half + 1) * LANES].astype(F32)
-    small_ref[...] = jnp.zeros_like(small_ref)
-    small_ref[0:rounds, 0:stabs] = coords_ref[...].astype(F32)
+    coords = coords_ref[...]
+    small_ref[0:rounds, 0:stabs] = (coords // BASE).astype(F32)
     for shot in range(shots):
         first = rounds * (1 + shot)
-        small_ref[first : first + rounds, 0:stabs] = bits_ref[shot].astype(F32)
-    turned = jnp.transpose(small_ref[...])
-    small_ref[...] = turned
-    small_ref[stabs : stabs + 1, :] = small_ref[stabs - 1 : stabs, :]
-    flip = row(flip_ref)
-    gain_attn = row(gain_attn_ref)
-    spot = lax.broadcasted_iota(jnp.int32, (rows, coord_rows), 1).astype(F32)
-    for pair in range(rounds // 2):
-        picks = []
-        for t in (2 * pair, 2 * pair + 1):
-            picks.append(jnp.where(small_ref[0:rows, t : t + 1] == spot, 1.0, 0.0))
-        base = dot(jnp.concatenate(picks, axis=0).astype(BF16), table_ref[...])
+        small_ref[first : first + rounds, 0:stabs] = (coords % BASE + BASE * bits_ref[shot]).astype(F32)
+    for item in range(parts):
+        shot, t = divmod(item, rounds)
+        where = pl.ds(shot * stabs * rounds + t, stabs, stride=rounds)
         for half in range(2):
-            t = 2 * pair + half
-            for shot in range(shots):
-                item = shot * rounds + t
-                lane = rounds * (1 + shot) + t
-                where = pl.ds(shot * stabs * rounds + t, stabs, stride=rounds)
-                own = jnp.concatenate([wide_ref[0, where, :], wide_ref[1, where, :]], axis=1)
-                start_ref[item, 0:stabs, :] = own
-                start_ref[item, stabs : stabs + 1, :] = own[stabs - 1 : stabs, :]
-                sign = 2.0 * small_ref[0:rows, lane : lane + 1] - 1.0
-                start = start_ref[item] + base[half * rows : (half + 1) * rows] + sign * flip
-                start_ref[item] = start
-                send1[item] = pack(norm_rows(start, gain_attn))
+            lane = t if half == 0 else rounds * (1 + shot) + t
+            loose_ref[item, half * rows : half * rows + stabs, :] = wide_ref[half, where, :]
+            loose_ref[item, half * rows + stabs : (half + 1) * rows, :] = small_ref[lane : lane + 1, :]
+        send1[item] = loose_ref[item].astype(BF16)
 
     pl.semaphore_wait(barrier, parts - 1 + blocks - 1)
 
@@ -176,12 +165,45 @@
         copy1(slot).start()
     recv1[0] = send1[me]
 
-    for index in range(6, INPUTS):
+    for index in range(3, INPUTS):
         load(index).wait()
+    flip = row(flip_ref)
+    gain_attn = row(gain_attn_ref)
+
+    def columns():
+        small_ref[...] = jnp.transpose(small_ref[...])
+        small_ref[stabs : stabs + 1, :] = small_ref[stabs - 1 : stabs, :]
+
+    def place(first, second):
+        low = small_ref[0:rows, second : second + 1]
+        flipped = low >= BASE
+        coord = small_ref[0:rows, first : first + 1] * BASE + low - jnp.where(flipped, float(BASE), 0.0)
+        return coord, jnp.where(flipped, 1.0, -1.0)
+
+    spot = lax.broadcasted_iota(jnp.int32, (rows, coord_rows), 1).astype(F32)
+
+    def look_up(coord):
+        picks = [jnp.where(one == spot, 1.0, 0.0) for one in coord]
+        return dot(jnp.concatenate(picks, axis=0).astype(BF16), table_ref[...])
+
+    columns()
+    for pair in range(rounds // 2):
+        base = look_up([place(t, rounds + t)[0] for t in (2 * pair, 2 * pair + 1)])
+        for half in range(2):
+            t = 2 * pair + half
+            for shot in range(shots):
+                item = shot * rounds + t
+                sign = place(t, rounds * (1 + shot) + t)[1]
+                for side in range(2):
+                    part = slice(side * LANES, (side + 1) * LANES)
+                    start_ref[item, 0:stabs, part] = loose_ref[item, side * rows : side * rows + stabs, :]
+                start_ref[item, stabs : stabs + 1, :] = start_ref[item, stabs - 1 : stabs, :]
+                start_ref[item] = start_ref[item] + base[half * rows : (half + 1) * rows] + sign * flip
+
     turned_ref[...] = jnp.transpose(wv_ref[...].astype(F32)).astype(BF16)
-    for group in range(groups):
-        pieces = []
-        for slot in range(group * GROUP, (group + 1) * GROUP):
+
+    for slots in ARRIVALS:
+        for slot in slots:
             if slot:
                 pltpu.make_async_remote_copy(
                     src_ref=send1.at[0],
@@ -191,9 +213,25 @@
                     device_id={"stab": peer(1)},
                     device_id_type=MESH,
                 ).wait_recv()
-            pieces.append(unpack(recv1[slot]))
-        normed = jnp.concatenate(pieces, axis=0).astype(BF16)
-        where = slice(group * gsize, (group + 1) * gsize)
+            message = recv1[slot].astype(F32)
+            index = slot - slots[0]
+            for half in range(2):
+                part = slice(half * LANES, (half + 1) * LANES)
+                mixed_ref[slot * rows : (slot + 1) * rows, part] = message[half * rows : (half + 1) * rows]
+            for half in range(2):
+                part = slice(half * LANES, (half + 1) * LANES)
+                spot_row = half * len(slots) + index
+                small_ref[spot_row : spot_row + 1, :] = mixed_ref[slot * rows + stabs : slot * rows + stabs + 1, part]
+            mixed_ref[slot * rows + stabs : (slot + 1) * rows, :] = mixed_ref[
+                slot * rows + stabs - 1 : (slot + 1) * rows - 1, :
+            ]
+        columns()
+        places = [place(index, len(slots) + index) for index in range(len(slots))]
+        sign = jnp.concatenate([jnp.broadcast_to(one[1], (rows, LANES)) for one in places], axis=0)
+        sign = jnp.concatenate([sign, sign], axis=1)
+        where = slice(slots[0] * rows, (slots[-1] + 1) * rows)
+        start = mixed_ref[where, :] + look_up([one[0] for one in places]) + sign * flip
+        normed = norm_rows(start, gain_attn).astype(BF16)
         q_ref[where, :] = dot(normed, wq_ref[...]).astype(BF16)
         k_ref[where, :] = dot(normed, wk_ref[...]).astype(BF16)
         n_ref[where, :] = normed
@@ -216,9 +254,9 @@
 
     scale = HD ** (-0.5) * math.log2(math.e)
     done = parts
-    for last in range(keys, 0, -QUERIES):
-        first = max(last - QUERIES, 0)
-        count = last - first
+    last = keys
+    for count in COUNTS:
+        first = last - count
         query = q_ref[first:last, :].astype(F32)
         head_of = lax.broadcasted_iota(jnp.int32, (count, width), 1) // HD
         for head in range(heads):
@@ -234,6 +272,7 @@
             send2[done] = pack(mixed_ref[done * rows : (done + 1) * rows, :])
             if done:
                 copy2(done, peer(hop(done))).start()
+        last = first
     recv2[me] = send2[0]
 
     gain_rec = row(gain_rec_ref)
@@ -357,8 +396,8 @@
 
     def finish(group, _):
         hiddens, afters = [], []
-        for index in range(GROUP):
-            item = group * GROUP + index
+        for index in range(FINISH):
+            item = group * FINISH + index
             shot = lax.div(item, rounds)
             hiddens.append(drive_ref[item] + decay_ref[item] * inc_ref[shot])
             afters.append(after_ref[item])
@@ -367,8 +406,8 @@
         ffn_in = norm_rows(after, gain_mlp).astype(BF16)
         inner = (jax.nn.silu(dot(ffn_in, wg_ref[...])) * dot(ffn_in, wu_ref[...])).astype(BF16)
         states = after + dot(inner, wdown_ref[...])
-        for index in range(GROUP):
-            item = group * GROUP + index
+        for index in range(FINISH):
+            item = group * FINISH + index
             first = lax.div(item, rounds) * (stabs * rounds) + lax.rem(item, rounds)
             for half in range(2):
                 wide_ref[half, pl.ds(first, stabs, stride=rounds), :] = states[
@@ -376,7 +415,7 @@
                 ]
         return 0
 
-    lax.fori_loop(0, groups, finish, 0)
+    lax.fori_loop(0, parts // FINISH, finish, 0)
     for half in range(2):
         out_ref[:, half * LANES : (half + 1) * LANES] = wide_ref[half].astype(BF16)
 
@@ -399,7 +438,8 @@
 def body(parts, blocks, *args):
     states_in = args[0]
     shots, rounds, stabs, width = states_in.shape
-    assert shots * rounds == parts
+    assert shots * rounds == parts and sum(COUNTS) == parts * (-(-stabs // 8) * 8)
+    assert sum(len(slots) for slots in ARRIVALS) == parts and args[3].shape[0] <= 256 * BASE
     assert len(args) == INPUTS
     rows = -(-stabs // 8) * 8
     flat = (jnp.transpose(states_in, (0, 2, 1, 3)).reshape(-1, width),) + args[1:]
@@ -415,6 +455,7 @@
         + [
             pltpu.VMEM((2, flat[0].shape[0], LANES), F32),
             pltpu.VMEM((LANES, LANES), F32),
+            pltpu.VMEM((parts,) + message, F32),
             pltpu.VMEM((parts, rows, width), F32),
             pltpu.VMEM((parts,) + message, BF16),
             pltpu.VMEM((parts,) + message, BF16),
@@ -423,7 +464,7 @@
             pltpu.VMEM((width // HD, HD + 16, parts * rows), BF16),
             pltpu.VMEM((parts * rows, width), BF16),
             pltpu.VMEM((width, width), BF16),
-            pltpu.VMEM((width, QUERIES), F32),
+            pltpu.VMEM((width, max(COUNTS)), F32),
             pltpu.VMEM((parts * rows, width), F32),
             pltpu.VMEM((parts,) + message, BF16),
             pltpu.VMEM((parts,) + message, BF16),

time: 63.4 us -> 66 us (1.041)
  Pallas kernels: 62.5 us -> 65 us
    pallas_call x1, Pallas kernels: 62.5 us -> 65 us  [body(): pl.pallas_call(functools.partial(kernel, parts, blocks), out_shape=pltpu....]
where the time goes in v4:
time: 66 us; the launch traced here: 65.7 us
  Pallas kernels  65 us (98%)
  local copies, waits for them, and re-layouts  0.72 us (1%)
    pallas_call x1, Pallas kernels, body(): pl.pallas_call(functools.partial(kernel, parts, blocks), out_shape=pltpu....  65 us

profile of v4, /device:TPU:24, one launch (start us, length us, event | category | flops | bytes accessed | tf_op | source)
XLA Modules:
  0.0 65.7 jit_solution(10480557675276729705)
XLA Ops:
  0.0 65.0 %shard_map.181 = bf16[624,256]{1,0:T(8,128)(2,1)S(1)} custom-call(bf16[624,256]{1,0:T(8,128)(2,1)} %bitcast.7, s32[2,8,39]{2,1,0:T(8,128)} %refs_1_.1, s32[8,39]{1,0:T(8,128)} %refs_2_.1, bf16[625,256]{1,0:T(8,128)(2,1)} %refs_3_.1, bf16[256]{0:T(256)(128)(2,1)} %refs_4_.1, bf16[256]{0:T(256)(128)(2,1)} %refs_5_.1, bf16[256,256]{1,0:T(8,128)(2,1)} %refs_6_.1, ...), custom_call_target="tpu_custom_call" | custom-call | tf_op jit(solution)/shard_map/pallas_call | solution.py:449
  65.0 0.7 %copy.21 = bf16[2,8,39,256]{3,1,2,0:T(8,128)(2,1)} copy(bf16[2,8,39,256]{3,1,2,0:T(8,128)(2,1)S(1)} %bitcast.6) | data formatting | bytes 638976

commit v5 on v3

--- a/solution.py
+++ b/solution.py
@@ -12,7 +12,8 @@
 LANES = 128
 GROUP = 4
 INPUTS = 19
-QUERIES = 256
+FINISH = 8
+COUNTS = (128, 256, 256)
 MESH = pl.DeviceIdType.MESH
 F32 = jnp.float32
 BF16 = jnp.bfloat16
@@ -199,10 +200,10 @@
         n_ref[where, :] = normed
     real = lax.rem(lax.broadcasted_iota(jnp.int32, (1, keys), 1), rows) < stabs
     values = jnp.where(real, dot_t(turned_ref[...], n_ref[...]), 0.0)
-    ones = jnp.where(real, jnp.ones((v_ref.shape[1] - HD, keys), F32), 0.0).astype(BF16)
-    for head in range(heads):
-        v_ref[head, 0:HD, :] = values[head * HD : (head + 1) * HD].astype(BF16)
-        v_ref[head, HD:, :] = ones
+    ones = jnp.where(real, jnp.ones((v_ref.shape[1] - 2 * HD, keys), F32), 0.0).astype(BF16)
+    for pair in range(heads // 2):
+        v_ref[pair, 0 : 2 * HD, :] = values[2 * HD * pair : 2 * HD * (pair + 1)].astype(BF16)
+        v_ref[pair, 2 * HD :, :] = ones
 
     def copy2(slot, target):
         return pltpu.make_async_remote_copy(
@@ -216,24 +217,29 @@
 
     scale = HD ** (-0.5) * math.log2(math.e)
     done = parts
-    for last in range(keys, 0, -QUERIES):
-        first = max(last - QUERIES, 0)
-        count = last - first
+    last = keys
+    for count in COUNTS:
+        first = last - count
         query = q_ref[first:last, :].astype(F32)
         head_of = lax.broadcasted_iota(jnp.int32, (count, width), 1) // HD
-        for head in range(heads):
-            mine = jnp.where(head_of == head, query, 0.0).astype(BF16)
-            scores = dot_t(k_ref[...], mine)
-            peak = jnp.max(scores, axis=0, keepdims=True)
-            weights = jnp.exp2((scores - peak) * scale).astype(BF16)
-            both = dot(v_ref[head], weights)
-            across_ref[head * HD : (head + 1) * HD, 0:count] = both[:HD] / both[HD : HD + 1]
+        spread = [jnp.where(head_of == head, query, 0.0) for head in range(heads)]
+        scores = dot_t(k_ref[...], jnp.concatenate(spread, axis=0).astype(BF16))
+        peak = jnp.max(scores, axis=0, keepdims=True)
+        weights = jnp.exp2((scores - peak) * scale).astype(BF16)
+        for head in range(0, heads, 2):
+            both = dot(v_ref[head // 2], weights[:, head * count : (head + 2) * count])
+            for index in range(2):
+                piece = both[:, index * count : (index + 1) * count]
+                across_ref[(head + index) * HD : (head + index + 1) * HD, 0:count] = (
+                    piece[index * HD : (index + 1) * HD] / piece[2 * HD : 2 * HD + 1]
+                )
         mixed_ref[first:last, :] = jnp.transpose(across_ref[:, 0:count])
         while done > 0 and (done - 1) * rows >= first:
             done -= 1
             send2[done] = pack(mixed_ref[done * rows : (done + 1) * rows, :])
             if done:
                 copy2(done, peer(hop(done))).start()
+        last = first
     recv2[me] = send2[0]
 
     gain_rec = row(gain_rec_ref)
@@ -357,8 +363,8 @@
 
     def finish(group, _):
         hiddens, afters = [], []
-        for index in range(GROUP):
-            item = group * GROUP + index
+        for index in range(FINISH):
+            item = group * FINISH + index
             shot = lax.div(item, rounds)
             hiddens.append(drive_ref[item] + decay_ref[item] * inc_ref[shot])
             afters.append(after_ref[item])
@@ -367,8 +373,8 @@
         ffn_in = norm_rows(after, gain_mlp).astype(BF16)
         inner = (jax.nn.silu(dot(ffn_in, wg_ref[...])) * dot(ffn_in, wu_ref[...])).astype(BF16)
         states = after + dot(inner, wdown_ref[...])
-        for index in range(GROUP):
-            item = group * GROUP + index
+        for index in range(FINISH):
+            item = group * FINISH + index
             first = lax.div(item, rounds) * (stabs * rounds) + lax.rem(item, rounds)
             for half in range(2):
                 wide_ref[half, pl.ds(first, stabs, stride=rounds), :] = states[
@@ -376,7 +382,7 @@
                 ]
         return 0
 
-    lax.fori_loop(0, groups, finish, 0)
+    lax.fori_loop(0, parts // FINISH, finish, 0)
     for half in range(2):
         out_ref[:, half * LANES : (half + 1) * LANES] = wide_ref[half].astype(BF16)
 
@@ -399,7 +405,7 @@
 def body(parts, blocks, *args):
     states_in = args[0]
     shots, rounds, stabs, width = states_in.shape
-    assert shots * rounds == parts
+    assert shots * rounds == parts and sum(COUNTS) == parts * (-(-stabs // 8) * 8)
     assert len(args) == INPUTS
     rows = -(-stabs // 8) * 8
     flat = (jnp.transpose(states_in, (0, 2, 1, 3)).reshape(-1, width),) + args[1:]
@@ -420,10 +426,10 @@
             pltpu.VMEM((parts,) + message, BF16),
             pltpu.VMEM((parts * rows, width), BF16),
             pltpu.VMEM((parts * rows, width), BF16),
-            pltpu.VMEM((width // HD, HD + 16, parts * rows), BF16),
+            pltpu.VMEM((width // (2 * HD), 2 * HD + 16, parts * rows), BF16),
             pltpu.VMEM((parts * rows, width), BF16),
             pltpu.VMEM((width, width), BF16),
-            pltpu.VMEM((width, QUERIES), F32),
+            pltpu.VMEM((width, max(COUNTS)), F32),
             pltpu.VMEM((parts * rows, width), F32),
             pltpu.VMEM((parts,) + message, BF16),
             pltpu.VMEM((parts,) + message, BF16),

time: 63.4 us -> 62.3 us (0.983)
  Pallas kernels: 62.5 us -> 61.3 us
    pallas_call x1, Pallas kernels: 62.5 us -> 61.3 us  [body(): pl.pallas_call(functools.partial(kernel, parts, blocks), out_shape=pltpu....]
where the time goes in v5:
time: 62.3 us; the launch traced here: 62.1 us
  Pallas kernels  61.3 us (98%)
  local copies, waits for them, and re-layouts  0.72 us (1%)
    pallas_call x1, Pallas kernels, body(): pl.pallas_call(functools.partial(kernel, parts, blocks), out_shape=pltpu....  61.3 us

profile of v5, /device:TPU:24, one launch (start us, length us, event | category | flops | bytes accessed | tf_op | source)
XLA Modules:
  0.0 62.1 jit_solution(17604570763270444607)
XLA Ops:
  0.0 61.3 %shard_map.181 = bf16[624,256]{1,0:T(8,128)(2,1)S(1)} custom-call(bf16[624,256]{1,0:T(8,128)(2,1)} %bitcast.7, s32[2,8,39]{2,1,0:T(8,128)} %refs_1_.1, s32[8,39]{1,0:T(8,128)} %refs_2_.1, bf16[625,256]{1,0:T(8,128)(2,1)} %refs_3_.1, bf16[256]{0:T(256)(128)(2,1)} %refs_4_.1, bf16[256]{0:T(256)(128)(2,1)} %refs_5_.1, bf16[256,256]{1,0:T(8,128)(2,1)} %refs_6_.1, ...), custom_call_target="tpu_custom_call" | custom-call | tf_op jit(solution)/shard_map/pallas_call | solution.py:415
  61.3 0.7 %copy.21 = bf16[2,8,39,256]{3,1,2,0:T(8,128)(2,1)} copy(bf16[2,8,39,256]{3,1,2,0:T(8,128)(2,1)S(1)} %bitcast.6) | data formatting | bytes 638976

commit v6 on v5

--- a/solution.py
+++ b/solution.py
@@ -12,7 +12,7 @@
 LANES = 128
 GROUP = 4
 INPUTS = 19
-FINISH = 8
+ARRIVALS = ((0, 1, 2, 3), (4, 5, 6, 7), (8, 9, 10, 11), (12, 13), (14, 15))
 COUNTS = (128, 256, 256)
 MESH = pl.DeviceIdType.MESH
 F32 = jnp.float32
@@ -84,7 +84,6 @@
     recv3,
     send4,
     recv4,
-    inc_ref,
     send1_sem,
     recv1_sem,
     send2_sem,
@@ -173,16 +172,16 @@
             device_id_type=MESH,
         )
 
-    for slot in range(parts - 1, 0, -1):
+    for slot in range(1, parts):
         copy1(slot).start()
     recv1[0] = send1[me]
 
     for index in range(6, INPUTS):
         load(index).wait()
     turned_ref[...] = jnp.transpose(wv_ref[...].astype(F32)).astype(BF16)
-    for group in range(groups):
+    for slots in ARRIVALS:
         pieces = []
-        for slot in range(group * GROUP, (group + 1) * GROUP):
+        for slot in slots:
             if slot:
                 pltpu.make_async_remote_copy(
                     src_ref=send1.at[0],
@@ -194,7 +193,7 @@
                 ).wait_recv()
             pieces.append(unpack(recv1[slot]))
         normed = jnp.concatenate(pieces, axis=0).astype(BF16)
-        where = slice(group * gsize, (group + 1) * gsize)
+        where = slice(slots[0] * rows, (slots[-1] + 1) * rows)
         q_ref[where, :] = dot(normed, wq_ref[...]).astype(BF16)
         k_ref[where, :] = dot(normed, wk_ref[...]).astype(BF16)
         n_ref[where, :] = normed
@@ -270,6 +269,32 @@
             decay_ref[item] = decay[part]
             drive_ref[item] = drive[part]
 
+    chunks = 2 * shots
+    step = blocks // chunks
+    shift = lax.rem(lax.axis_index("shot"), step)
+    my_chunk = lax.div(block, step)
+    owner = lax.rem(block, step) == shift
+
+    def copy3(chunk):
+        return pltpu.make_async_remote_copy(
+            src_ref=send3.at[chunk],
+            dst_ref=recv3.at[block],
+            send_sem=send3_sem.at[chunk],
+            recv_sem=recv3_sem.at[block],
+            device_id={"round": chunk * step + shift},
+            device_id_type=MESH,
+        )
+
+    def copy4(target):
+        return pltpu.make_async_remote_copy(
+            src_ref=send4.at[target],
+            dst_ref=recv4.at[my_chunk],
+            send_sem=send4_sem.at[target],
+            recv_sem=recv4_sem.at[my_chunk],
+            device_id={"round": target},
+            device_id_type=MESH,
+        )
+
     for shot in range(shots):
         state = drive_ref[shot * rounds]
         product = decay_ref[shot * rounds]
@@ -283,42 +308,15 @@
         for half in range(2):
             part = slice(half * LANES, (half + 1) * LANES)
             send3[2 * shot + half] = jnp.concatenate([product[:, part], state[:, part]], axis=0).astype(BF16)
-
-    chunks = 2 * shots
-    step = blocks // chunks
-    shift = lax.rem(lax.axis_index("shot"), step)
-    my_chunk = lax.div(block, step)
-    owner = lax.rem(block, step) == shift
-
-    def copy3(chunk):
-        return pltpu.make_async_remote_copy(
-            src_ref=send3.at[chunk],
-            dst_ref=recv3.at[block],
-            send_sem=send3_sem.at[chunk],
-            recv_sem=recv3_sem.at[block],
-            device_id={"round": chunk * step + shift},
-            device_id_type=MESH,
-        )
-
-    def copy4(target):
-        return pltpu.make_async_remote_copy(
-            src_ref=send4.at[target],
-            dst_ref=recv4.at[my_chunk],
-            send_sem=send4_sem.at[target],
-            recv_sem=recv4_sem.at[my_chunk],
-            device_id={"round": target},
-            device_id_type=MESH,
-        )
-
-    for chunk in range(chunks):
-
-        @pl.when(block != chunk * step + shift)
-        def _():
-            copy3(chunk).start()
-
-        @pl.when(block == chunk * step + shift)
-        def _():
-            recv3[block] = send3[chunk]
+            chunk = 2 * shot + half
+
+            @pl.when(block != chunk * step + shift)
+            def _():
+                copy3(chunk).start()
+
+            @pl.when(block == chunk * step + shift)
+            def _():
+                recv3[block] = send3[chunk]
 
     @pl.when(owner)
     def _():
@@ -343,46 +341,35 @@
             entering = wide[:rows] * entering + wide[rows:]
         recv4[my_chunk] = send4[block]
 
-    for chunk in range(chunks):
-
-        @pl.when(block != chunk * step + shift)
-        def _():
-            pltpu.make_async_remote_copy(
-                src_ref=send4.at[0],
-                dst_ref=recv4.at[chunk],
-                send_sem=send4_sem.at[0],
-                recv_sem=recv4_sem.at[chunk],
-                device_id={"round": chunk * step + shift},
-                device_id_type=MESH,
-            ).wait_recv()
-
-        part = slice((chunk % 2) * LANES, (chunk % 2 + 1) * LANES)
-        inc_ref[chunk // 2, :, part] = recv4[chunk].astype(F32)[:rows]
-
     gain_mlp = row(gain_mlp_ref)
-
-    def finish(group, _):
-        hiddens, afters = [], []
-        for index in range(FINISH):
-            item = group * FINISH + index
-            shot = lax.div(item, rounds)
-            hiddens.append(drive_ref[item] + decay_ref[item] * inc_ref[shot])
-            afters.append(after_ref[item])
-        hidden = jnp.concatenate(hiddens, axis=0).astype(BF16)
-        after = jnp.concatenate(afters, axis=0) + dot(hidden, wr_ref[...])
+    for shot in range(shots):
+        halves = []
+        for chunk in (2 * shot, 2 * shot + 1):
+
+            @pl.when(block != chunk * step + shift)
+            def _():
+                pltpu.make_async_remote_copy(
+                    src_ref=send4.at[0],
+                    dst_ref=recv4.at[chunk],
+                    send_sem=send4_sem.at[0],
+                    recv_sem=recv4_sem.at[chunk],
+                    device_id={"round": chunk * step + shift},
+                    device_id_type=MESH,
+                ).wait_recv()
+
+            halves.append(recv4[chunk].astype(F32)[:rows])
+        entering = jnp.concatenate(halves, axis=1)
+        items = range(shot * rounds, (shot + 1) * rounds)
+        hidden = [drive_ref[item] + decay_ref[item] * entering for item in items]
+        after = jnp.concatenate([after_ref[item] for item in items], axis=0)
+        after = after + dot(jnp.concatenate(hidden, axis=0).astype(BF16), wr_ref[...])
         ffn_in = norm_rows(after, gain_mlp).astype(BF16)
         inner = (jax.nn.silu(dot(ffn_in, wg_ref[...])) * dot(ffn_in, wu_ref[...])).astype(BF16)
         states = after + dot(inner, wdown_ref[...])
-        for index in range(FINISH):
-            item = group * FINISH + index
-            first = lax.div(item, rounds) * (stabs * rounds) + lax.rem(item, rounds)
+        for t in range(rounds):
+            where = pl.ds(shot * stabs * rounds + t, stabs, stride=rounds)
             for half in range(2):
-                wide_ref[half, pl.ds(first, stabs, stride=rounds), :] = states[
-                    index * rows : index * rows + stabs, half * LANES : (half + 1) * LANES
-                ]
-        return 0
-
-    lax.fori_loop(0, parts // FINISH, finish, 0)
+                wide_ref[half, where, :] = states[t * rows : t * rows + stabs, half * LANES : (half + 1) * LANES]
     for half in range(2):
         out_ref[:, half * LANES : (half + 1) * LANES] = wide_ref[half].astype(BF16)
 
@@ -405,7 +392,8 @@
 def body(parts, blocks, *args):
     states_in = args[0]
     shots, rounds, stabs, width = states_in.shape
-    assert shots * rounds == parts and sum(COUNTS) == parts * (-(-stabs // 8) * 8)
+    assert shots * rounds == parts and sum(map(len, ARRIVALS)) == parts
+    assert sum(COUNTS) == parts * (-(-stabs // 8) * 8)
     assert len(args) == INPUTS
     rows = -(-stabs // 8) * 8
     flat = (jnp.transpose(states_in, (0, 2, 1, 3)).reshape(-1, width),) + args[1:]
@@ -440,7 +428,6 @@
             pltpu.VMEM((blocks,) + message, BF16),
             pltpu.VMEM((blocks, -(-rows // 16) * 16, LANES), BF16),
             pltpu.VMEM((2 * shots, -(-rows // 16) * 16, LANES), BF16),
-            pltpu.VMEM((shots, rows, width), F32),
             dma((parts,)),
             dma((parts,)),
             dma((parts,)),

time: 62.3 us -> 61 us (0.979)
  Pallas kernels: 61.3 us -> 60.1 us
    pallas_call x1, Pallas kernels: 61.3 us -> 60.1 us  [body(): pl.pallas_call(functools.partial(kernel, parts, blocks), out_shape=pltpu....]
where the time goes in v6:
time: 61 us; the launch traced here: 60.8 us
  Pallas kernels  60.1 us (99%)
  local copies, waits for them, and re-layouts  0.72 us (1%)
    pallas_call x1, Pallas kernels, body(): pl.pallas_call(functools.partial(kernel, parts, blocks), out_shape=pltpu....  60.1 us

profile of v6, /device:TPU:24, one launch (start us, length us, event | category | flops | bytes accessed | tf_op | source)
XLA Modules:
  0.0 60.8 jit_solution(4834093224812302859)
XLA Ops:
  0.0 60.1 %shard_map.181 = bf16[624,256]{1,0:T(8,128)(2,1)S(1)} custom-call(bf16[624,256]{1,0:T(8,128)(2,1)} %bitcast.7, s32[2,8,39]{2,1,0:T(8,128)} %refs_1_.1, s32[8,39]{1,0:T(8,128)} %refs_2_.1, bf16[625,256]{1,0:T(8,128)(2,1)} %refs_3_.1, bf16[256]{0:T(256)(128)(2,1)} %refs_4_.1, bf16[256]{0:T(256)(128)(2,1)} %refs_5_.1, bf16[256,256]{1,0:T(8,128)(2,1)} %refs_6_.1, ...), custom_call_target="tpu_custom_call" | custom-call | tf_op jit(solution)/shard_map/pallas_call | solution.py:403
  60.1 0.7 %copy.21 = bf16[2,8,39,256]{3,1,2,0:T(8,128)(2,1)} copy(bf16[2,8,39,256]{3,1,2,0:T(8,128)(2,1)S(1)} %bitcast.6) | data formatting | bytes 638976

commit v7 on v6

--- a/solution.py
+++ b/solution.py
@@ -10,10 +10,10 @@
 
 HD = 32
 LANES = 128
-GROUP = 4
 INPUTS = 19
 ARRIVALS = ((0, 1, 2, 3), (4, 5, 6, 7), (8, 9, 10, 11), (12, 13), (14, 15))
 COUNTS = (128, 256, 256)
+GATES = ((12, 13, 14, 15), (8, 9, 10, 11), (4, 5, 6, 7), (2, 3), (0, 1))
 MESH = pl.DeviceIdType.MESH
 F32 = jnp.float32
 BF16 = jnp.bfloat16
@@ -101,8 +101,6 @@
     rows = start_ref.shape[1]
     coord_rows = table_ref.shape[0]
     heads = width // HD
-    gsize = GROUP * rows
-    groups = parts // GROUP
     keys = parts * rows
     me = lax.axis_index("stab")
     block = lax.axis_index("round")
@@ -179,6 +177,16 @@
     for index in range(6, INPUTS):
         load(index).wait()
     turned_ref[...] = jnp.transpose(wv_ref[...].astype(F32)).astype(BF16)
+    def turn(first, last):
+        lane = first + lax.broadcasted_iota(jnp.int32, (1, last - first), 1)
+        real = lax.rem(lane, rows) < stabs
+        values = jnp.where(real, dot_t(turned_ref[...], n_ref[first:last, :]), 0.0)
+        ones = jnp.where(real, jnp.ones((v_ref.shape[1] - 2 * HD, last - first), F32), 0.0).astype(BF16)
+        for pair in range(heads // 2):
+            v_ref[pair, 0 : 2 * HD, first:last] = values[2 * HD * pair : 2 * HD * (pair + 1)].astype(BF16)
+            v_ref[pair, 2 * HD :, first:last] = ones
+
+    ready = 0
     for slots in ARRIVALS:
         pieces = []
         for slot in slots:
@@ -197,12 +205,10 @@
         q_ref[where, :] = dot(normed, wq_ref[...]).astype(BF16)
         k_ref[where, :] = dot(normed, wk_ref[...]).astype(BF16)
         n_ref[where, :] = normed
-    real = lax.rem(lax.broadcasted_iota(jnp.int32, (1, keys), 1), rows) < stabs
-    values = jnp.where(real, dot_t(turned_ref[...], n_ref[...]), 0.0)
-    ones = jnp.where(real, jnp.ones((v_ref.shape[1] - 2 * HD, keys), F32), 0.0).astype(BF16)
-    for pair in range(heads // 2):
-        v_ref[pair, 0 : 2 * HD, :] = values[2 * HD * pair : 2 * HD * (pair + 1)].astype(BF16)
-        v_ref[pair, 2 * HD :, :] = ones
+        upto = (slots[-1] + 1) * rows // LANES * LANES
+        if upto - ready >= 2 * LANES or upto == keys:
+            turn(ready, upto)
+            ready = upto
 
     def copy2(slot, target):
         return pltpu.make_async_remote_copy(
@@ -242,9 +248,9 @@
     recv2[me] = send2[0]
 
     gain_rec = row(gain_rec_ref)
-    for group in range(groups - 1, -1, -1):
+    for slots in GATES:
         pieces, starts = [], []
-        for slot in range(group * GROUP, (group + 1) * GROUP):
+        for slot in slots:
             item = peer(hop(slot))
             if slot:
                 pltpu.make_async_remote_copy(
@@ -262,8 +268,8 @@
         rec_in = norm_rows(after, gain_rec).astype(BF16)
         decay = jax.nn.sigmoid(dot(rec_in, wd_ref[...]) + row(bias_ref))
         drive = (1.0 - decay) * dot(rec_in, wi_ref[...])
-        for index in range(GROUP):
-            item = peer(hop(group * GROUP + index))
+        for index, slot in enumerate(slots):
+            item = peer(hop(slot))
             part = slice(index * rows, (index + 1) * rows)
             after_ref[item] = after[part]
             decay_ref[item] = decay[part]
@@ -393,7 +399,7 @@
     states_in = args[0]
     shots, rounds, stabs, width = states_in.shape
     assert shots * rounds == parts and sum(map(len, ARRIVALS)) == parts
-    assert sum(COUNTS) == parts * (-(-stabs // 8) * 8)
+    assert sum(map(len, GATES)) == parts and sum(COUNTS) == parts * (-(-stabs // 8) * 8)
     assert len(args) == INPUTS
     rows = -(-stabs // 8) * 8
     flat = (jnp.transpose(states_in, (0, 2, 1, 3)).reshape(-1, width),) + args[1:]

time: 61 us -> 61.3 us (level)
  no operation moved by 1% of the time
where the time goes in v7:
time: 61.3 us; the launch traced here: 61.1 us
  Pallas kernels  60.4 us (99%)
  local copies, waits for them, and re-layouts  0.72 us (1%)
    pallas_call x1, Pallas kernels, body(): pl.pallas_call(functools.partial(kernel, parts, blocks), out_shape=pltpu....  60.4 us

profile of v7, /device:TPU:24, one launch (start us, length us, event | category | flops | bytes accessed | tf_op | source)
XLA Modules:
  0.0 61.1 jit_solution(17108418453583151111)
XLA Ops:
  0.0 60.4 %shard_map.181 = bf16[624,256]{1,0:T(8,128)(2,1)S(1)} custom-call(bf16[624,256]{1,0:T(8,128)(2,1)} %bitcast.7, s32[2,8,39]{2,1,0:T(8,128)} %refs_1_.1, s32[8,39]{1,0:T(8,128)} %refs_2_.1, bf16[625,256]{1,0:T(8,128)(2,1)} %refs_3_.1, bf16[256]{0:T(256)(128)(2,1)} %refs_4_.1, bf16[256]{0:T(256)(128)(2,1)} %refs_5_.1, bf16[256,256]{1,0:T(8,128)(2,1)} %refs_6_.1, ...), custom_call_target="tpu_custom_call" | custom-call | tf_op jit(solution)/shard_map/pallas_call | solution.py:409
  60.4 0.7 %copy.21 = bf16[2,8,39,256]{3,1,2,0:T(8,128)(2,1)} copy(bf16[2,8,39,256]{3,1,2,0:T(8,128)(2,1)S(1)} %bitcast.6) | data formatting | bytes 638976

commit v8 on v6

--- a/solution.py
+++ b/solution.py
@@ -310,7 +310,7 @@
             send3[2 * shot + half] = jnp.concatenate([product[:, part], state[:, part]], axis=0).astype(BF16)
             chunk = 2 * shot + half
 
-            @pl.when(block != chunk * step + shift)
+            @pl.when((block != chunk * step + shift) & (block < blocks - 1))
             def _():
                 copy3(chunk).start()
 
@@ -328,6 +328,12 @@
             @pl.when(block != source)
             def _():
                 copy4(source).start()
+
+            if source == blocks - 1:
+                break
+
+            @pl.when(block != source)
+            def _():
                 pltpu.make_async_remote_copy(
                     src_ref=send3.at[0],
                     dst_ref=recv3.at[source],
@@ -378,7 +384,7 @@
         copy2(slot, peer(1)).wait_send()
     for chunk in range(chunks):
 
-        @pl.when(block != chunk * step + shift)
+        @pl.when((block != chunk * step + shift) & (block < blocks - 1))
         def _():
             copy3(chunk).wait_send()
 

time: 61 us -> 60.9 us (level)
  no operation moved by 1% of the time
where the time goes in v8:
time: 60.9 us; the launch traced here: 60.8 us
  Pallas kernels  60 us (99%)
  local copies, waits for them, and re-layouts  0.72 us (1%)
    pallas_call x1, Pallas kernels, body(): pl.pallas_call(functools.partial(kernel, parts, blocks), out_shape=pltpu....  60 us

profile of v8, /device:TPU:24, one launch (start us, length us, event | category | flops | bytes accessed | tf_op | source)
XLA Modules:
  0.0 60.8 jit_solution(11592280083986729765)
XLA Ops:
  0.0 60.0 %shard_map.181 = bf16[624,256]{1,0:T(8,128)(2,1)S(1)} custom-call(bf16[624,256]{1,0:T(8,128)(2,1)} %bitcast.7, s32[2,8,39]{2,1,0:T(8,128)} %refs_1_.1, s32[8,39]{1,0:T(8,128)} %refs_2_.1, bf16[625,256]{1,0:T(8,128)(2,1)} %refs_3_.1, bf16[256]{0:T(256)(128)(2,1)} %refs_4_.1, bf16[256]{0:T(256)(128)(2,1)} %refs_5_.1, bf16[256,256]{1,0:T(8,128)(2,1)} %refs_6_.1, ...), custom_call_target="tpu_custom_call" | custom-call | tf_op jit(solution)/shard_map/pallas_call | solution.py:409
  60.0 0.7 %copy.21 = bf16[2,8,39,256]{3,1,2,0:T(8,128)(2,1)} copy(bf16[2,8,39,256]{3,1,2,0:T(8,128)(2,1)S(1)} %bitcast.6) | data formatting | bytes 638976
